TPU v7x, 256 devices: a whole 4x4x8 slice. The times are simulated.
256 devices in a mesh: band: 32 (over z, y), mp: 8 (over x, core).
Axes of the slice: x: 4, y: 4, z: 8, core: 2. Of those that a mesh axis runs over, the one named last changes fastest.
Arguments:
- skip_features: bfloat16 [192, 48, 512], P('band'), may hold values from -6 to 6
- deep_features: bfloat16 [96, 24, 2048], P('band'), may hold values from -6 to 6
- top_gains: float32 [2, 2, 512], replicated, may hold values from 0.5 to 1.5
- top_heads_in: bfloat16 [2, 512, 3, 512], P(None, 'band', None, 'mp'), may hold values from -0.25 to 0.25
- top_heads_out: bfloat16 [2, 512, 512], P(None, 'mp', 'band'), may hold values from -0.25 to 0.25
- top_hidden_in: bfloat16 [2, 512, 2048], P(None, 'band', 'mp'), may hold values from -0.25 to 0.25
- top_hidden_out: bfloat16 [2, 2048, 512], P(None, 'mp', 'band'), may hold values from -0.125 to 0.125
- top_offsets: float32 [2, 16, 11, 23], P(None, 'mp'), may hold values from -4 to 400
- deep_gains: float32 [2, 2048], replicated, may hold values from 0.5 to 1.5
- deep_offsets: float32 [64, 5, 11], P('mp'), may hold values from -4 to 400
- deep_heads_in: bfloat16 [2048, 3, 2048], P('band', None, 'mp'), may hold values from -0.125 to 0.125
- deep_heads_out: bfloat16 [2048, 2048], P('mp', 'band'), may hold values from -0.125 to 0.125
- deep_hidden_in: bfloat16 [2048, 8192], P('band', 'mp'), may hold values from -0.125 to 0.125
- deep_hidden_out: bfloat16 [8192, 2048], P('mp', 'band'), may hold values from -0.0625 to 0.0625
- expand_weight: bfloat16 [2048, 4, 512], P('band', None, 'mp'), may hold values from -0.125 to 0.125
Outputs:
- decoded: bfloat16 [192, 48, 512], P('band')
All inputs are finite; a program needn't handle non-finite values.
Results may differ from a plain program's by a relative error of at most 0.03.
Values may be sent and summed in bfloat16 or wider, within the bound.
A program may use at most 64 MiB of HBM per device.

v0:
```python
import jax
import jax.numpy as jnp
import numpy as np
from jax import lax
from jax.sharding import PartitionSpec as P

HS = 32
WH = 6
WW = 12
DWH = 3
DWW = 6


eps = 1e-05


def extended(x, sides, width):
    for axis, dim in sides:
        size, length = (lax.axis_size(axis), x.shape[dim])
        up = [(i, (i + 1) % size) for i in range(size - 1)]
        down = [(j, i) for i, j in up]
        last = lax.slice_in_dim(x, length - width, length, axis=dim)
        leading = lax.slice_in_dim(x, 0, width, axis=dim)
        before = lax.ppermute(last, axis, up)
        after = lax.ppermute(leading, axis, down)
        x = jnp.concatenate([before, x, after], axis=dim)
    return x


def norm_rows(values, scales):
    floats = values.astype(jnp.float32)
    centred = floats - jnp.mean(floats, axis=-1, keepdims=True)
    spread = jnp.mean(centred * centred, axis=-1, keepdims=True)
    return (centred * lax.rsqrt(spread + eps) * scales).astype(jnp.bfloat16)


def to_windows(values, window_rows, window_cols):
    count_rows = values.shape[0] // window_rows
    count_cols = values.shape[1] // window_cols
    trailing = values.shape[2:]
    shaped = values.reshape((count_rows, window_rows, count_cols, window_cols) + trailing)
    shaped = jnp.moveaxis(shaped, 2, 1)
    return shaped.reshape((count_rows, count_cols, window_rows * window_cols) + trailing)


def from_windows(values, window_rows, window_cols):
    count_rows, count_cols = (values.shape[0], values.shape[1])
    trailing = values.shape[3:]
    shaped = values.reshape((count_rows, count_cols, window_rows, window_cols) + trailing)
    shaped = jnp.moveaxis(shaped, 1, 2)
    return shaped.reshape((count_rows * window_rows, count_cols * window_cols) + trailing)


def offset_hot(extent):
    places = np.arange(extent)
    marks = (
        places[:, None, None] - places[None, :, None] + extent - 1
        == np.arange(2 * extent - 1)[None, None, :]
    )
    return jnp.asarray(marks.astype(np.float32))


def position_bias(offsets, window_rows, window_cols):
    expanded = jnp.einsum(
        "hab,ija,klb->hikjl",
        offsets,
        offset_hot(window_rows),
        offset_hot(window_cols),
        precision=lax.Precision.HIGHEST,
    )
    return expanded.reshape(offsets.shape[0], window_rows * window_cols, window_rows * window_cols)


def window_attend(queries, key_heads, value_heads, query_rows, key_rows, window_cols, additive):
    query_win = to_windows(queries, query_rows, window_cols)
    key_win = to_windows(key_heads, key_rows, window_cols)
    value_win = to_windows(value_heads, key_rows, window_cols)
    scale_factor = queries.shape[-1] ** (-0.5)
    scores = (
        jnp.einsum("abnhs,abmhs->abhnm", query_win, key_win, preferred_element_type=jnp.float32)
        * scale_factor
        + additive
    )
    highest = jnp.max(scores, axis=-1, keepdims=True)
    weights = jnp.exp(scores - highest)
    attention = (weights / jnp.sum(weights, axis=-1, keepdims=True)).astype(jnp.bfloat16)
    blended = jnp.einsum(
        "abhnm,abmhs->abnhs", attention, value_win, preferred_element_type=jnp.float32
    ).astype(jnp.bfloat16)
    return from_windows(blended, query_rows, window_cols)


def add_block(operand, piece_rows):
    return jnp.dot(
        operand, piece_rows.reshape(piece_rows.shape[0], -1), preferred_element_type=jnp.float32
    )


def local(
    skip_features,
    deep_features,
    top_gains,
    top_heads_in,
    top_heads_out,
    top_hidden_in,
    top_hidden_out,
    top_offsets,
    deep_gains,
    deep_offsets,
    deep_heads_in,
    deep_heads_out,
    deep_hidden_in,
    deep_hidden_out,
    expand_weight,
):
    deep_rows, deep_cols, deep_width = deep_features.shape
    deep_local = deep_heads_in.shape[2]
    deep_tokens = deep_rows * deep_cols
    expand_local = expand_weight.shape[2]
    deep_normed = norm_rows(deep_features, deep_gains[0]).reshape(deep_tokens, deep_width)
    deep_pre_heads = add_block(
        deep_normed, lax.all_gather(deep_heads_in, "band", axis=0, tiled=True)
    )
    deep_projected = deep_pre_heads.astype(jnp.bfloat16).reshape(
        deep_rows, deep_cols, 3, deep_local // HS, HS
    )
    deep_additive = position_bias(deep_offsets, DWH, DWW)[None, None]
    deep_blended = window_attend(
        deep_projected[:, :, 0],
        deep_projected[:, :, 1],
        deep_projected[:, :, 2],
        DWH,
        DWH,
        DWW,
        deep_additive,
    )
    deep_flat_mix = deep_blended.reshape(deep_tokens, deep_local)
    deep_partial = jnp.dot(
        deep_flat_mix,
        lax.all_gather(deep_heads_out, "band", axis=1, tiled=True),
        preferred_element_type=jnp.float32,
    )
    deep_attn_delta = lax.psum(deep_partial.astype(jnp.bfloat16), "mp").astype(jnp.float32)
    deep_middle = (
        deep_features.astype(jnp.float32)
        + deep_attn_delta.reshape(deep_rows, deep_cols, deep_width)
    ).astype(jnp.bfloat16)
    deep_normed_two = norm_rows(deep_middle, deep_gains[1]).reshape(deep_tokens, deep_width)
    deep_pre = add_block(
        deep_normed_two, lax.all_gather(deep_hidden_in, "band", axis=0, tiled=True)
    )
    deep_activated = jax.nn.gelu(deep_pre, approximate=False).astype(jnp.bfloat16)
    deep_mlp_partial = jnp.dot(
        deep_activated,
        lax.all_gather(deep_hidden_out, "band", axis=1, tiled=True),
        preferred_element_type=jnp.float32,
    )
    deep_mlp_delta = lax.psum(deep_mlp_partial.astype(jnp.bfloat16), "mp").astype(jnp.float32)
    deep_out = (
        deep_middle.astype(jnp.float32) + deep_mlp_delta.reshape(deep_rows, deep_cols, deep_width)
    ).astype(jnp.bfloat16)
    flat_deep = deep_out.reshape(deep_tokens, deep_width)
    grown = add_block(flat_deep, lax.all_gather(expand_weight, "band", axis=0, tiled=True)).astype(
        jnp.bfloat16
    )
    grown = lax.all_gather(grown.reshape(deep_tokens, 4, expand_local), "mp", axis=2, tiled=True)
    top_width = grown.shape[2]
    grown = (
        grown.reshape(deep_rows, deep_cols, 2, 2, top_width)
        .transpose(0, 2, 1, 3, 4)
        .reshape(2 * deep_rows, 2 * deep_cols, top_width)
    )
    current = (skip_features.astype(jnp.float32) + grown.astype(jnp.float32)).astype(jnp.bfloat16)
    rows_here, lon_here = (current.shape[0], current.shape[1])
    token_count = rows_here * lon_here
    half_rows = WH // 2
    half_cols = WW // 2
    band_count = lax.axis_size("band")
    band_index = lax.axis_index("band")
    for section_index in range(2):
        shifted = section_index == 1
        offsets_here = top_offsets[section_index]
        local_heads = offsets_here.shape[0]
        local_width = local_heads * HS
        bias_full = position_bias(offsets_here, WH, WW)
        normed_top = norm_rows(current, top_gains[section_index, 0])
        source = normed_top
        if shifted:
            source = extended(normed_top, (("band", 0),), half_rows)
        source_rows = source.shape[0]
        source_flat = source.reshape(source_rows * lon_here, top_width)
        projected = add_block(
            source_flat, lax.all_gather(top_heads_in[section_index], "band", axis=0, tiled=True)
        ).astype(jnp.bfloat16)
        projected = projected.reshape(source_rows, lon_here, 3, local_heads, HS)
        if not shifted:
            blended = window_attend(
                projected[:, :, 0],
                projected[:, :, 1],
                projected[:, :, 2],
                WH,
                WH,
                WW,
                bias_full[None, None],
            )
        else:
            queries = projected[half_rows : half_rows + rows_here, :, 0]
            key_ext = projected[:, :, 1]
            value_ext = projected[:, :, 2]
            global_row = (
                band_index * rows_here
                - half_rows
                + jnp.arange(rows_here + 2 * half_rows, dtype=jnp.int32)
            )
            valid_key = ((global_row >= 0) & (global_row < rows_here * band_count)).astype(
                jnp.float32
            )
            queries = jnp.roll(queries, -half_cols, axis=1)
            key_ext = jnp.roll(key_ext, -half_cols, axis=1)
            value_ext = jnp.roll(value_ext, -half_cols, axis=1)
            valid_grid = jnp.broadcast_to(valid_key[:, None], (valid_key.shape[0], lon_here))
            valid_win = to_windows(valid_grid, WH, WW)
            split_at = half_rows * WW
            bias_pair = jnp.stack([bias_full[:, split_at:], bias_full[:, :split_at]])[:, None]
            additive = bias_pair + (valid_win[:, :, None, None, :] - 1.0) * 1e30
            blended = window_attend(queries, key_ext, value_ext, half_rows, WH, WW, additive)
            blended = jnp.roll(blended, half_cols, axis=1)
        mix_flat = blended.reshape(token_count, local_width)
        top_partial = jnp.dot(
            mix_flat,
            lax.all_gather(top_heads_out[section_index], "band", axis=1, tiled=True),
            preferred_element_type=jnp.float32,
        )
        attn_delta = lax.psum(top_partial.astype(jnp.bfloat16), "mp").astype(jnp.float32)
        after_attn = (
            current.astype(jnp.float32) + attn_delta.reshape(rows_here, lon_here, top_width)
        ).astype(jnp.bfloat16)
        normed_mlp = norm_rows(after_attn, top_gains[section_index, 1]).reshape(
            token_count, top_width
        )
        top_pre = add_block(
            normed_mlp, lax.all_gather(top_hidden_in[section_index], "band", axis=0, tiled=True)
        )
        top_activated = jax.nn.gelu(top_pre, approximate=False).astype(jnp.bfloat16)
        mlp_partial = jnp.dot(
            top_activated,
            lax.all_gather(top_hidden_out[section_index], "band", axis=1, tiled=True),
            preferred_element_type=jnp.float32,
        )
        mlp_delta = lax.psum(mlp_partial.astype(jnp.bfloat16), "mp").astype(jnp.float32)
        current = (
            after_attn.astype(jnp.float32) + mlp_delta.reshape(rows_here, lon_here, top_width)
        ).astype(jnp.bfloat16)
    return current


def solution(mesh):
    placed = (
        P("band", None, None),
        P("band", None, None),
        P(),
        P(None, "band", None, "mp"),
        P(None, "mp", "band"),
        P(None, "band", "mp"),
        P(None, "mp", "band"),
        P(None, "mp", None, None),
        P(),
        P("mp", None, None),
        P("band", None, "mp"),
        P("mp", "band"),
        P("band", "mp"),
        P("mp", "band"),
        P("band", None, "mp"),
    )
    return jax.shard_map(
        local, mesh=mesh, in_specs=placed, out_specs=P("band", None, None), check_vma=False
    )
```

profile of v0, /device:TPU:1, one launch (start us, length us, event | category | flops | bytes accessed | tf_op | source)
XLA Modules:
  0.0 996.6 jit_solution(17879072740191407457)
XLA Ops:
  6.5 0.7 all-gather.14.cloned.1.call-update
  7.3 0.7 all-gather.16.cloned.1.call-update
  8.1 1.1 convert_reduce_fusion.5
  9.1 1.2 fusion.42
  10.3 1.2 convolution_bitcast_fusion.5
  11.5 1.2 convolution_bitcast_fusion.2
  12.7 0.4 copy.287
  13.1 0.8 reshape.373
  13.9 0.8 fusion.307
  14.7 1.1 fusion.44
  15.9 73.9 %all-gather.14.cloned.1.call-done = bf16[2048,3,256]{2,0,1:T(8,128)(2,1)} async-done(((bf16[64,3,256]{2,0,1:T(8,128)(2,1)}), bf16[2048,3,256]{2,0,1:T(8,128)(2,1)}) %all-gather.14.cloned.1.call-update) | async-done | bytes 3145744 | tf_op jit(solution)/shard_map/all_gather | solution.py:122
  89.7 3.2 copy.224
  92.9 1.7 convolution_convert_fusion.10
  94.7 1.3 reshape.308
  96.2 1.2 fusion.310
  97.4 0.3 fusion.12
  97.9 66.8 %all-gather.16.cloned.1.call-done = bf16[256,2048]{0,1:T(8,128)(2,1)} async-done(((bf16[256,64]{0,1:T(8,128)(2,1)}), bf16[256,2048]{0,1:T(8,128)(2,1)}) %all-gather.16.cloned.1.call-update) | async-done | bytes 1048592 | tf_op jit(solution)/shard_map/all_gather | solution.py:140
  164.7 2.4 convolution_convert_fusion
  167.2 0.5 all-gather.18.cloned.1.call-update
  167.8 0.5 all-gather.20.cloned.1.call-update
  168.4 0.5 all-gather.22.cloned.1.call-update
  169.0 0.3 convolution_bitcast_fusion.4
  169.4 0.3 convolution_bitcast_fusion.3
  169.7 1.8 convolution_bitcast_fusion.1
  171.5 1.8 convolution_bitcast_fusion
  173.3 34.5 %all-gather = bf16[1,512,3,64]{3,1,2,0:T(8,128)(2,1)S(1)} all-gather(bf16[1,16,3,64]{3,1,2,0:T(8,128)(2,1)S(1)} %get-tuple-element.28), channel_id=2, replica_groups=mesh['band'=32,'mp'=8] {'band'}, dimensions={1}, use_global_device_ids=true | all-gather | bytes 202752 | tf_op jit(solution)/shard_map/all_gather | solution.py:193
  208.1 0.7 copy.288
  209.0 33.5 %all-gather.1 = bf16[1,64,512]{1,2,0:T(8,128)(2,1)S(1)} all-gather(bf16[1,64,16]{1,2,0:T(8,128)(2,1)S(1)} %get-tuple-element.42), channel_id=3, replica_groups=mesh['band'=32,'mp'=8] {'band'}, dimensions={2}, use_global_device_ids=true | all-gather | bytes 67584 | tf_op jit(solution)/shard_map/all_gather | solution.py:231
  242.4 1.1 convert_reduce_fusion.4
  244.0 71.5 %all-gather.18.cloned.1.call-done = bf16[2048,1024]{1,0:T(8,128)(2,1)} async-done(((bf16[64,1024]{1,0:T(8,128)(2,1)}), bf16[2048,1024]{1,0:T(8,128)(2,1)}) %all-gather.18.cloned.1.call-update) | async-done | bytes 4194320 | tf_op jit(solution)/shard_map/all_gather | solution.py:150
  315.5 81.9 %all-gather.20.cloned.1.call-done = bf16[1024,2048]{0,1:T(8,128)(2,1)} async-done(((bf16[1024,64]{0,1:T(8,128)(2,1)}), bf16[1024,2048]{0,1:T(8,128)(2,1)}) %all-gather.20.cloned.1.call-update) | async-done | bytes 4194320 | tf_op jit(solution)/shard_map/all_gather | solution.py:155
  397.4 6.9 convolution_convert_fusion.1
  404.4 69.7 %all-gather.22.cloned.1.call-done = bf16[2048,4,64]{2,1,0:T(4,128)(2,1)} async-done(((bf16[64,4,64]{2,1,0:T(4,128)(2,1)}), bf16[2048,4,64]{2,1,0:T(4,128)(2,1)}) %all-gather.22.cloned.1.call-update) | async-done | bytes 1048592 | tf_op jit(solution)/shard_map/all_gather | solution.py:163
  474.1 2.9 copy.240
  477.1 63.7 %all-reduce.9.cloned.1.call-done = bf16[3,24,2048]{2,1,0:T(8,128)(2,1)} async-done(((bf16[3,24,2048]{2,1,0:T(8,128)(2,1)}), bf16[3,24,2048]{2,1,0:T(8,128)(2,1)}) %all-reduce.9.cloned.1.call-update) | async-done | bytes 294928 | tf_op jit(solution)/shard_map/psum | solution.py:158
  540.8 1.1 fusion.46
  541.9 0.5 convolution_convert_fusion.12
  542.6 15.9 %all_gather.47 = bf16[72,4,512]{0,1,2:T(4,128)(2,1)S(1)} all-gather(bf16[72,4,64]{0,1,2:T(4,128)(2,1)S(1)} %copy.241), channel_id=1, replica_groups=mesh['band'=32,'mp'=8] {'mp'}, dimensions={2}, use_global_device_ids=true | all-gather | bytes 331776 | tf_op jit(solution)/shard_map/all_gather | solution.py:166
  558.5 0.3 copy.242
  558.9 0.5 copy.243
  559.3 0.4 reshape.351
  560.7 0.3 reshape.323
  562.9 1.0 convolution_convert_fusion.5
  564.1 39.6 %all-gather.2 = bf16[1,512,256]{2,1,0:T(8,128)(2,1)S(1)} all-gather(bf16[1,16,256]{2,1,0:T(8,128)(2,1)S(1)} %get-tuple-element.32), channel_id=4, replica_groups=mesh['band'=32,'mp'=8] {'band'}, dimensions={1}, use_global_device_ids=true | all-gather | bytes 270336 | tf_op jit(solution)/shard_map/all_gather | solution.py:242
  603.7 35.9 %all-gather.3 = bf16[1,256,512]{1,2,0:T(8,128)(2,1)S(1)} all-gather(bf16[1,256,16]{1,2,0:T(8,128)(2,1)S(1)} %get-tuple-element.34), channel_id=5, replica_groups=mesh['band'=32,'mp'=8] {'band'}, dimensions={2}, use_global_device_ids=true | all-gather | bytes 270336 | tf_op jit(solution)/shard_map/all_gather | solution.py:247
  639.6 1.1 convert_reduce_fusion.2
  641.2 1.8 convolution_convert_fusion.4
  643.1 81.7 %all-reduce.13.cloned.1.call-done = bf16[6,48,512]{2,1,0:T(8,128)(2,1)} async-done(((bf16[6,48,512]{2,1,0:T(8,128)(2,1)}), bf16[6,48,512]{2,1,0:T(8,128)(2,1)}) %all-reduce.13.cloned.1.call-update) | async-done | bytes 294928 | tf_op jit(solution)/shard_map/psum | solution.py:250
  724.8 1.1 convert_reduce_fusion.1
  726.4 2.9 collective-permute-start
  729.3 1.3 collective-permute-start.1
  730.6 37.3 %all-gather.4 = bf16[1,512,3,64]{3,1,2,0:T(8,128)(2,1)S(1)} all-gather(bf16[1,16,3,64]{3,1,2,0:T(8,128)(2,1)S(1)} %get-tuple-element.27), channel_id=6, replica_groups=mesh['band'=32,'mp'=8] {'band'}, dimensions={1}, use_global_device_ids=true | all-gather | bytes 202752 | tf_op jit(solution)/shard_map/all_gather | solution.py:193
  768.3 32.7 %all-gather.5 = bf16[1,64,512]{1,2,0:T(8,128)(2,1)S(1)} all-gather(bf16[1,64,16]{1,2,0:T(8,128)(2,1)S(1)} %get-tuple-element.41), channel_id=7, replica_groups=mesh['band'=32,'mp'=8] {'band'}, dimensions={2}, use_global_device_ids=true | all-gather | bytes 67584 | tf_op jit(solution)/shard_map/all_gather | solution.py:231
  801.1 0.4 convolution_convert_fusion.6
  801.5 0.8 reshape.335
  805.0 1.3 fusion.13
  807.2 1.0 convolution_convert_fusion.3
  808.2 35.0 %all-gather.6 = bf16[1,512,256]{2,1,0:T(8,128)(2,1)S(1)} all-gather(bf16[1,16,256]{2,1,0:T(8,128)(2,1)S(1)} %get-tuple-element.31), channel_id=8, replica_groups=mesh['band'=32,'mp'=8] {'band'}, dimensions={1}, use_global_device_ids=true | all-gather | bytes 270336 | tf_op jit(solution)/shard_map/all_gather | solution.py:242
  843.2 36.9 %all-gather.7 = bf16[1,256,512]{1,2,0:T(8,128)(2,1)S(1)} all-gather(bf16[1,256,16]{1,2,0:T(8,128)(2,1)S(1)} %get-tuple-element.33), channel_id=9, replica_groups=mesh['band'=32,'mp'=8] {'band'}, dimensions={2}, use_global_device_ids=true | all-gather | bytes 270336 | tf_op jit(solution)/shard_map/all_gather | solution.py:247
  880.1 10.0 %all-reduce.15.cloned.1.call-done = bf16[6,48,512]{2,1,0:T(8,128)(2,1)} async-done(((bf16[6,48,512]{2,1,0:T(8,128)(2,1)}), bf16[6,48,512]{2,1,0:T(8,128)(2,1)}) %all-reduce.15.cloned.1.call-update) | async-done | bytes 294928 | tf_op jit(solution)/shard_map/psum | solution.py:234
  890.1 1.1 convert_reduce_fusion
  891.7 1.8 convolution_convert_fusion.2
  893.5 94.8 %all-reduce.17.cloned.1.call-done = bf16[6,48,512]{2,1,0:T(8,128)(2,1)} async-done(((bf16[6,48,512]{2,1,0:T(8,128)(2,1)}), bf16[6,48,512]{2,1,0:T(8,128)(2,1)}) %all-reduce.17.cloned.1.call-update) | async-done | bytes 294928 | tf_op jit(solution)/shard_map/psum | solution.py:250
  988.3 1.8 fusion.50
  (131 shorter events, 9.8 us)
Async XLA Ops:
  6.5 3.8 copy-start
  6.5 83.2 %all-gather.14.cloned.1.call-start = ((), (), s32[]{:S(2)}) async-start(), calls=%async_computation | async-start | bytes 3244032 | tf_op jit(solution)/shard_map/all_gather | solution.py:122
  7.3 157.5 %all-gather.16.cloned.1.call-start = ((), (), s32[]{:S(2)}) async-start(), calls=%async_computation.1 | async-start | bytes 1081344 | tf_op jit(solution)/shard_map/all_gather | solution.py:140
  8.0 234.4 %all-reduce.7.cloned.1.call-start = ((), (), s32[]{:S(2)}) async-start(), calls=%async_computation.2 | async-start | bytes 589824 | tf_op jit(solution)/shard_map/psum | solution.py:143
  94.7 74.3 %copy-start.5 = (bf16[2,16,3,64]{3,1,2,0:T(8,128)(2,1)S(1)}, bf16[2,16,3,64]{3,1,2,0:T(8,128)(2,1)}, u32[]{:S(2)}) copy-start(bf16[2,16,3,64]{3,1,2,0:T(8,128)(2,1)} %param.24) | copy-start | bytes 36868
  94.7 74.3 %copy-start.6 = (f32[2,2,11,23]{3,1,2,0:T(2,128)S(1)}, f32[2,2,11,23]{3,1,2,0:T(2,128)}, u32[]{:S(2)}) copy-start(f32[2,2,11,23]{3,1,2,0:T(2,128)} %param.28) | copy-start | bytes 12148
  94.7 74.3 %copy-start.7 = (bf16[2,16,256]{2,1,0:T(8,128)(2,1)S(1)}, bf16[2,16,256]{2,1,0:T(8,128)(2,1)}, u32[]{:S(2)}) copy-start(bf16[2,16,256]{2,1,0:T(8,128)(2,1)} %param.26) | copy-start | bytes 49156
  94.7 74.3 %copy-start.2 = (f32[12,12,23,1]{2,1,3,0:T(8,128)S(1)}, f32[12,12,23,1]{2,1,3,0:T(8,128)}, u32[]{:S(2)}) copy-start(f32[12,12,23,1]{2,1,3,0:T(8,128)} %constant.41) | copy-start | bytes 39748
  96.0 73.7 %copy-start.4 = (f32[6,6,11,1,1]{2,1,0,4,3:T(8,128)S(1)}, f32[6,6,11,1,1]{2,1,0,4,3:T(8,128)}, u32[]{:S(2)}) copy-start(f32[6,6,11,1,1]{2,1,0,4,3:T(8,128)} %constant.42) | copy-start | bytes 4756
  96.1 77.2 %copy-start.9 = (bf16[2,64,16]{1,2,0:T(8,128)(2,1)S(1)}, bf16[2,64,16]{1,2,0:T(8,128)(2,1)}, u32[]{:S(2)}) copy-start(bf16[2,64,16]{1,2,0:T(8,128)(2,1)} %param.25) | copy-start | bytes 12292
  97.7 144.7 %copy-start.1 = (bf16[3,24,2048]{2,1,0:T(8,128)(2,1)S(1)}, bf16[3,24,2048]{2,1,0:T(8,128)(2,1)}, u32[]{:S(2)}) copy-start(bf16[3,24,2048]{2,1,0:T(8,128)(2,1)} %param.22) | copy-start | bytes 884740
  167.2 148.4 %all-gather.18.cloned.1.call-start = ((), (), s32[]{:S(2)}) async-start(), calls=%async_computation.3 | async-start | bytes 4325376 | tf_op jit(solution)/shard_map/all_gather | solution.py:150
  167.7 229.7 %all-gather.20.cloned.1.call-start = ((), (), s32[]{:S(2)}) async-start(), calls=%async_computation.4 | async-start | bytes 4325376 | tf_op jit(solution)/shard_map/all_gather | solution.py:155
  168.3 305.8 %all-gather.22.cloned.1.call-start = ((), (), s32[]{:S(2)}) async-start(), calls=%async_computation.6 | async-start | bytes 2162688 | tf_op jit(solution)/shard_map/all_gather | solution.py:163
  168.9 371.9 %all-reduce.9.cloned.1.call-start = ((), (), s32[]{:S(2)}) async-start(), calls=%async_computation.5 | async-start | bytes 589824 | tf_op jit(solution)/shard_map/psum | solution.py:158
  397.4 7.0 copy-start.10
  404.3 235.3 %all-reduce.11.cloned.1.call-start = ((), (), s32[]{:S(2)}) async-start(), calls=%async_computation.7 | async-start | bytes 589824 | tf_op jit(solution)/shard_map/psum | solution.py:234
  477.0 82.7 %copy-start.3 = (bf16[6,48,512]{2,1,0:T(8,128)(2,1)S(1)}, bf16[6,48,512]{2,1,0:T(8,128)(2,1)}, u32[]{:S(2)}) copy-start(bf16[6,48,512]{2,1,0:T(8,128)(2,1)} %param.21) | copy-start | bytes 884740
  560.1 3.7 copy-start.8
  563.8 161.0 %all-reduce.13.cloned.1.call-start = ((), (), s32[]{:S(2)}) async-start(), calls=%async_computation.8 | async-start | bytes 589824 | tf_op jit(solution)/shard_map/psum | solution.py:250
  643.0 247.1 %all-reduce.15.cloned.1.call-start = ((), (), s32[]{:S(2)}) async-start(), calls=%async_computation.9 | async-start | bytes 589824 | tf_op jit(solution)/shard_map/psum | solution.py:234
  726.4 74.6 %collective-permute-start = (bf16[3,48,512]{2,1,0:T(8,128)(2,1)S(1)}, bf16[3,48,512]{2,1,0:T(8,128)(2,1)S(1)}, u32[]{:S(2)}, u32[]{:S(2)}) collective-permute-start(bf16[3,48,512]{2,1,0:T(8,128)(2,1)S(1)} %get-tuple-element.23), channel_id=1, source_target_pairs={{0,8},{8,16},{16,24},{24,32},{32,40},{40,48},{48,56},{56,64},{64,7... | collective-permute-start | bytes 442376 | tf_op jit(solution)/shard_map/ppermute | solution.py:24
  729.3 71.7 %collective-permute-start.1 = (bf16[3,48,512]{2,1,0:T(8,128)(2,1)S(1)}, bf16[3,48,512]{2,1,0:T(8,128)(2,1)S(1)}, u32[]{:S(2)}, u32[]{:S(2)}) collective-permute-start(bf16[3,48,512]{2,1,0:T(8,128)(2,1)S(1)} %get-tuple-element.24), channel_id=1, source_target_pairs={{8,0},{16,8},{24,16},{32,24},{40,32},{48,40},{56,48},{64,56},{72,6... | collective-permute-start | bytes 442376 | tf_op jit(solution)/shard_map/ppermute | solution.py:25
  808.2 180.2 %all-reduce.17.cloned.1.call-start = ((), (), s32[]{:S(2)}) async-start(), calls=%async_computation.10 | async-start | bytes 589824 | tf_op jit(solution)/shard_map/psum | solution.py:250
Sparse Core Ops, SparseCore 0:
  9.9 79.7 all-gather.13
  92.3 72.3 all-gather.15
  167.3 65.1 all-reduce.6
  235.3 80.1 all-gather.17
  318.3 79.0 all-gather.19
  400.2 73.9 all-gather.21
  476.6 64.1 all-reduce.8
  564.0 62.4 all-reduce.10
  643.1 81.6 all-reduce.12
  808.3 81.8 all-reduce.14
  893.6 94.6 all-reduce.16
where the time goes:
time: 999 us; the launch traced here: 997 us
  waiting for transfers between devices  617 us (62%)
  blocking collectives  301 us (30%)
  matrix products  27.9 us (3%)
  local copies, waits for them, and re-layouts  17.4 us (2%)
  between operations  14.1 us (1%)
  other arithmetic  14 us (1%)
    psum x2, waiting for transfers between devices, local(): lax.psum(mlp_partial.astype(jnp.bfloat16), 'mp').astype(jnp.float32)  177 us
    all_gather x1, waiting for transfers between devices, local(): lax.all_gather(deep_hidden_out, 'band', axis=1, tiled=True)  81.9 us
    all_gather x2, blocking collectives, local(): lax.all_gather(top_hidden_in[section_index], 'band', axis=0, tiled=True)  74.6 us
    all_gather x1, waiting for transfers between devices, local(): lax.all_gather(deep_heads_in, 'band', axis=0, tiled=True)  73.9 us
    all_gather x2, blocking collectives, local(): lax.all_gather(top_hidden_out[section_index], 'band', axis=1, tiled=True)  72.8 us
    all_gather x2, blocking collectives, local(): lax.all_gather(top_heads_in[section_index], 'band', axis=0, tiled=True)  71.9 us
    all_gather x1, waiting for transfers between devices, local(): lax.all_gather(deep_hidden_in, 'band', axis=0, tiled=True)  71.5 us
    all_gather x1, waiting for transfers between devices, local(): lax.all_gather(expand_weight, 'band', axis=0, tiled=True)  69.7 us
  transfers between devices with their start and end apart: 13, of which 9 were waited for; matrix products, arithmetic and copies ran while one was open for 3% of the time, Pallas kernels for 0%

commit v1 on v0

v1 whole, which is shorter than its diff:
```python
import functools

import jax
import jax.numpy as jnp
import numpy as np
from jax import lax
from jax.experimental import pallas as pl
from jax.experimental.pallas import tpu as pltpu
from jax.sharding import PartitionSpec as P

BF = jnp.bfloat16
F32 = jnp.float32
EPS = 1e-05
NEG = -1e30
T = 80
USED = 72
EXT = 400
SCALE = 32 ** (-0.5)
STAGES = ((0, 1024), (1024, 1024), (2048, 1280))
MESH = pl.DeviceIdType.MESH

PIECES = (
    (-1, 0, 3, 3, 0, 12, 80, 48),
    (1, 0, 0, 3, 0, 12, 128, 48),
    (0, -1, 0, 6, 6, 6, 176, 48),
    (0, 1, 0, 6, 0, 6, 224, 48),
    (-1, -1, 3, 3, 6, 6, 272, 32),
    (-1, 1, 3, 3, 0, 6, 304, 32),
    (1, -1, 0, 3, 6, 6, 336, 32),
    (1, 1, 0, 3, 0, 6, 368, 32),
)


@functools.lru_cache(None)
def tables():
    key_row = np.zeros(EXT, np.int32)
    key_col = np.zeros(EXT, np.int32)
    key_ok = np.zeros(EXT, bool)
    key_step = np.zeros(EXT, np.int32)
    t = np.arange(USED)
    key_row[:USED], key_col[:USED], key_ok[:USED] = t // 12, t % 12, True
    take = np.zeros((EXT, T), np.float32)
    for band_step, x_step, r0, nr, c0, nc, off, _ in PIECES:
        p = np.arange(nr * nc)
        r, c = r0 + p // nc, c0 + p % nc
        key_row[off : off + nr * nc] = r + 6 * band_step
        key_col[off : off + nr * nc] = c + 12 * x_step
        key_ok[off : off + nr * nc] = True
        key_step[off : off + nr * nc] = band_step
        take[off + p, r * 12 + c] = 1.0
    keys = np.zeros((8, EXT), np.int32)
    keys[0] = np.where(key_ok, 23 * key_row + key_col, -100000)
    keys[1] = key_step
    q_row, q_col = np.zeros(T, np.int32), np.zeros(T, np.int32)
    q_row[:USED], q_col[:USED] = t // 12, t % 12
    same = ((q_row >= 3)[:, None] == (key_row >= 3)[None]) & (
        (q_col >= 6)[:, None] == (key_col >= 6)[None]
    )
    mask_one = np.where(same & key_ok[None], 0.0, NEG).astype(np.float32)
    mask_zero = np.where((np.arange(T) < USED)[None], 0.0, NEG).astype(np.float32)
    mask_zero = np.broadcast_to(mask_zero, (T, T)).copy()
    deep_row, deep_col = np.zeros(T, np.int32), np.zeros(T, np.int32)
    deep_row[:USED], deep_col[:USED] = t // 24, t % 24
    deep_keys = np.full((8, T), -100000, np.int32)
    deep_keys[:, :USED] = 11 * deep_row[:USED] + deep_col[:USED] % 6
    ok = (np.arange(T) < USED)[None] & ((deep_col // 6)[:, None] == (deep_col // 6)[None])
    mask_deep = np.where(ok, 0.0, NEG).astype(np.float32)
    grow = np.zeros((4, T, T), np.float32)
    part = np.zeros((T, 4), np.float32)
    i, k = t // 12, t % 12
    for w in range(4):
        grow[w, t, (i // 2) * 24 + 6 * w + k // 2] = 1.0
    part[t, 2 * (i % 2) + k % 2] = 1.0
    part = np.repeat(part[:, :, None], 64, axis=2).reshape(T, 256)
    pick = np.zeros((4, T, 288), np.float32)
    place = np.zeros((288, 4 * T), np.float32)
    for w in range(4):
        pick[w, t, i * 48 + 12 * w + k] = 1.0
        place[i * 48 + 12 * w + k, w * T + t] = 1.0
    heads = np.zeros((8 * T, 256), np.float32)
    for h in range(8):
        heads[h * T : (h + 1) * T, h * 32 : (h + 1) * 32] = 1.0
    return (
        keys,
        mask_one,
        mask_zero,
        deep_keys,
        mask_deep,
        grow.astype(jnp.bfloat16),
        part,
        pick.astype(jnp.bfloat16),
        place.astype(jnp.bfloat16),
        take[T:].astype(jnp.bfloat16),
        heads.astype(jnp.bfloat16),
    )


def dot(a, b):
    return jnp.dot(a, b, preferred_element_type=F32)


def dot_t(a, b):
    return lax.dot_general(a, b, (((1,), (1,)), ((), ())), preferred_element_type=F32)


def thirds(values):
    first = values.astype(BF)
    rest = values - first.astype(F32)
    second = rest.astype(BF)
    third = (rest - second.astype(F32)).astype(BF)
    return jnp.concatenate([first, second, third], axis=0)


def norm_rows(values, scales):
    centred = values - jnp.mean(values, axis=-1, keepdims=True)
    spread = jnp.mean(centred * centred, axis=-1, keepdims=True)
    return (centred * lax.rsqrt(spread + EPS) * scales).astype(BF)


def gelu(values):
    return values * 0.5 * (1.0 + lax.erf(values * (0.5**0.5)))


def attend(q, k, v, bias, heads):
    stacked = jnp.concatenate([q] * 8, axis=0) * heads
    scores = dot_t(stacked, k) * SCALE + bias
    weights = jnp.exp(scores - jnp.max(scores, axis=-1, keepdims=True))
    weights = (weights * (1.0 / jnp.sum(weights, axis=-1, keepdims=True))).astype(BF)
    mixed = dot(weights, v) * heads.astype(F32)
    total = mixed[0:T]
    for h in range(1, 8):
        total = total + mixed[h * T : (h + 1) * T]
    return total.astype(BF)


def kernel(
    skip_ref,
    deep_ref,
    top_gain_ref,
    deep_gain_ref,
    top_tab_ref,
    deep_tab_ref,
    deep_pack_ref,
    top_pack_ref,
    keys_ref,
    mask_one_ref,
    mask_zero_ref,
    deep_keys_ref,
    mask_deep_ref,
    grow_ref,
    part_ref,
    pick_ref,
    place_ref,
    take_ref,
    heads_ref,
    out_ref,
    dw,
    tw,
    tabs,
    deep_raw,
    deep_bias,
    top_raw,
    bias_zero,
    bias_one,
    deep_x,
    rs_send,
    rs_recv,
    mids,
    grow_send,
    grow_recv,
    swap_send,
    swap_recv,
    halo_send,
    halo,
    fin,
    s_o1y,
    r_o1y,
    s_o1z,
    r_o1z,
    s_o2z,
    r_o2z,
    s_o2y,
    r_o2y,
    s_tz,
    r_tz,
    s_ty,
    r_ty,
    s_tx,
    r_tx,
    s_tab,
    r_tab,
    s_rs,
    r_rs,
    s_ag,
    r_ag,
    s_grow,
    r_grow,
    s_swap,
    r_swap,
    s_halo,
    r_halo,
    s_fin,
    r_fin,
):
    band = lax.axis_index("band")
    m = lax.axis_index("mp")
    z, y, x, c = band // 4, band % 4, m // 2, m % 2
    zs = [lax.rem(z + d, 8) for d in range(8)]
    ys = [lax.rem(y + d, 4) for d in range(4)]
    xs = [lax.rem(x + d, 4) for d in range(4)]
    ms = [lax.rem(m + d, 8) for d in range(8)]
    other = 1 - c

    def at_z(d):
        return {"band": zs[d % 8] * 4 + y, "mp": m}

    def at_y(d):
        return {"band": z * 4 + ys[d % 4], "mp": m}

    def at_m(d):
        return {"band": band, "mp": ms[d % 8]}

    def at_x(d, core):
        return {"band": band, "mp": xs[d % 4] * 2 + core}

    def at_piece(band_step, x_step):
        return {"band": lax.rem(band + band_step + 32, 32), "mp": xs[x_step % 4] * 2 + c}

    barrier = pltpu.get_barrier_semaphore()
    greeted = [at_z(1), at_z(7)] + [at_y(d) for d in (1, 2, 3)] + [at_m(d) for d in range(1, 8)]
    greeted += [at_piece(b, d) for b in (-1, 1) for d in (-1, 0, 1)]
    for who in greeted:
        pl.semaphore_signal(barrier, inc=1, device_id=who, device_id_type=MESH)

    sends = []

    def copy(src, dst, ss, rs, who):
        return pltpu.make_async_remote_copy(
            src_ref=src, dst_ref=dst, send_sem=ss, recv_sem=rs, device_id=who, device_id_type=MESH
        )

    def send(src, dst, ss, rs, who):
        cp = copy(src, dst, ss, rs, who)
        cp.start()
        sends.append(cp)

    def await_at(dst, ss, rs, who):
        copy(dst, dst, ss, rs, who).wait_recv()

    for half in range(2):
        dw[z, y, half] = deep_pack_ref[32 * half : 32 * half + 32, :]
    tw[x, z, y] = top_pack_ref[...]
    tabs[x] = top_tab_ref[...]
    pl.semaphore_wait(barrier, len(greeted))

    def o1(zz, s):
        lo, n = STAGES[s]
        return dw.at[zz, :, 0, :, pl.ds(lo, n)]

    def o1_own(yy, s):
        lo, n = STAGES[s]
        return dw.at[z, yy, 0, :, pl.ds(lo, n)]

    def o2(zz, yy, s):
        lo, n = STAGES[s]
        return dw.at[zz, yy, 1, :, pl.ds(lo, n)]

    def slot(order, way, dist):
        most = 4 if order == 1 else 3
        return dist - 1 if way > 0 else most + dist - 1

    def limit(order, way):
        return 4 if (order == 1) == (way > 0) else 3

    def hop(order, s, way, dist):
        origin = zs[(-way * (dist - 1)) % 8]
        k = slot(order, way, dist)
        if order == 1:
            send(o1(origin, s), o1(origin, s), s_o1z.at[s, k], r_o1z.at[s, k], at_z(way))
        else:
            send(o2(origin, y, s), o2(origin, y, s), s_o2z.at[s, k], r_o2z.at[s, k], at_z(way))

    def spread(s, origin, k):
        for d in (1, 2, 3):
            send(o2(origin, y, s), o2(origin, y, s), s_o2y.at[s, k, d - 1], r_o2y.at[s, k, d - 1], at_y(d))

    def begin(s):
        for d in (1, 2, 3):
            send(o1_own(y, s), o1_own(y, s), s_o1y.at[s, d - 1], r_o1y.at[s, d - 1], at_y(d))
        hop(2, s, 1, 1)
        hop(2, s, -1, 1)
        spread(s, z, 0)

    def begin_z(s):
        for d in (1, 2, 3):
            await_at(o1_own(ys[(-d) % 4], s), s_o1y.at[s, d - 1], r_o1y.at[s, d - 1], at_y(d))
        hop(1, s, 1, 1)
        hop(1, s, -1, 1)

    def step(s, dist):
        for order in (1, 2):
            for way in (1, -1):
                if dist > limit(order, way):
                    continue
                origin = zs[(-way * dist) % 8]
                k = slot(order, way, dist)
                if order == 1:
                    await_at(o1(origin, s), s_o1z.at[s, k], r_o1z.at[s, k], at_z(way))
                else:
                    await_at(o2(origin, y, s), s_o2z.at[s, k], r_o2z.at[s, k], at_z(way))
                if dist < limit(order, way):
                    hop(order, s, way, dist + 1)
                if order == 2:
                    spread(s, origin, k + 1)

    def finish(s):
        for way, most in ((0, 1), (1, 3), (-1, 4)):
            for dist in range(1, most + 1):
                origin = zs[(-way * dist) % 8]
                k = 0 if way == 0 else slot(2, way, dist) + 1
                for d in (1, 2, 3):
                    await_at(
                        o2(origin, ys[(-d) % 4], s),
                        s_o2y.at[s, k, d - 1],
                        r_o2y.at[s, k, d - 1],
                        at_y(d),
                    )

    def top_hop(way, dist):
        origin = zs[(-way * (dist - 1)) % 8]
        k = slot(1, way, dist)
        send(tw.at[x, origin, y], tw.at[x, origin, y], s_tz.at[k], r_tz.at[k], at_z(way))

    def top_step(dist):
        for way in (1, -1):
            if dist > limit(1, way):
                continue
            origin = zs[(-way * dist) % 8]
            k = slot(1, way, dist)
            await_at(tw.at[x, origin, y], s_tz.at[k], r_tz.at[k], at_z(way))
            if dist < limit(1, way):
                top_hop(way, dist + 1)

    def top_y():
        for d in (1, 2, 3):
            send(tw.at[x, :, y], tw.at[x, :, y], s_ty.at[d - 1], r_ty.at[d - 1], at_y(d))

    def layer_of(xx, layer):
        return tw.at[xx, :, :, :, pl.ds(768 * layer, 768)]

    def top_x():
        for d in (1, 2, 3):
            yy = ys[(-d) % 4]
            await_at(tw.at[x, :, yy], s_ty.at[d - 1], r_ty.at[d - 1], at_y(d))
        for layer in range(2):
            for d in (1, 3, 2):
                ss, rs = s_tx.at[layer, d - 1], r_tx.at[layer, d - 1]
                send(layer_of(x, layer), layer_of(x, layer), ss, rs, at_x(d, c))

    def top_ready(layer):
        for d in (1, 2, 3):
            ss, rs = s_tx.at[layer, d - 1], r_tx.at[layer, d - 1]
            await_at(layer_of(xs[(-d) % 4], layer), ss, rs, at_x(d, c))

    def scatter(which):
        for d in range(1, 8):
            ss, rs = s_rs.at[which, d - 1], r_rs.at[which, d - 1]
            send(rs_send.at[which, ms[d]], rs_recv.at[which, m], ss, rs, at_m(d))
        rs_recv[which, m] = rs_send[which, m]

    def gathered_sum(which):
        for d in range(1, 8):
            ss, rs = s_rs.at[which, d - 1], r_rs.at[which, d - 1]
            await_at(rs_recv.at[which, ms[(-d) % 8]], ss, rs, at_m(d))
        total = rs_recv[which, 0].astype(F32)
        for j in range(1, 8):
            total = total + rs_recv[which, j].astype(F32)
        return total

    def share(which):
        for d in range(1, 8):
            ss, rs = s_ag.at[which, d - 1], r_ag.at[which, d - 1]
            send(mids.at[which, m], mids.at[which, m], ss, rs, at_m(d))

    def shared(which):
        for d in range(1, 8):
            ss, rs = s_ag.at[which, d - 1], r_ag.at[which, d - 1]
            await_at(mids.at[which, ms[(-d) % 8]], ss, rs, at_m(d))

    def swap(which, partial):
        swap_send[which] = partial.astype(BF)
        send(swap_send.at[which], swap_recv.at[which], s_swap.at[which], r_swap.at[which], at_x(0, other))

    def swapped(which):
        await_at(swap_recv.at[which], s_swap.at[which], r_swap.at[which], at_x(0, other))
        return swap_send[which].astype(F32) + swap_recv[which].astype(F32)

    top_hop(1, 1)
    top_hop(-1, 1)
    begin(0)
    for d in (1, 2, 3):
        send(tabs.at[x], tabs.at[x], s_tab.at[d - 1], r_tab.at[d - 1], at_x(d, c))

    for i in range(3):
        deep_x[24 * i : 24 * i + 24, :] = deep_ref[i].astype(F32)
    deep_x[USED:T, :] = jnp.zeros((T - USED, 2048), F32)
    begin_z(0)
    normed = norm_rows(deep_x[...], deep_gain_ref[0:1, :])

    deep_tab = thirds(deep_tab_ref[...])
    deep_iota = lax.broadcasted_iota(jnp.int32, (128, T), 0) + deep_keys_ref[0:1, :]

    def deep_row(n, carry):
        r = n // 24
        col = n - 24 * r
        want = (r + 2) * 11 + lax.rem(col, 6) + 5
        hot = jnp.where(deep_iota == want, 1.0, 0.0).astype(BF)
        got = dot(deep_tab, hot)
        deep_raw[n] = got[0:8] + got[8:16] + got[16:24]
        return carry

    lax.fori_loop(0, USED, deep_row, 0)
    top_step(1)
    step(0, 1)
    begin(1)
    for h in range(8):
        deep_bias[h * T : h * T + USED, :] = deep_raw[:, h, :] + mask_deep_ref[0:USED, :]
        deep_bias[h * T + USED : (h + 1) * T, :] = mask_deep_ref[USED:T, :]
    top_step(2)
    step(0, 2)
    begin_z(1)
    top_step(3)
    top_step(4)
    top_y()

    for d in (1, 2, 3):
        await_at(tabs.at[xs[(-d) % 4]], s_tab.at[d - 1], r_tab.at[d - 1], at_x(d, c))
    top_tab = thirds(tabs[...].reshape(32, 256))
    top_iota = lax.broadcasted_iota(jnp.int32, (256, EXT), 0) + keys_ref[0:1, :]

    def top_row(n, carry):
        i = n // 12
        want = (i + 5) * 23 + (n - 12 * i) + 11
        hot = jnp.where(top_iota == want, 1.0, 0.0).astype(BF)
        got = dot(top_tab, hot)
        top_raw[n] = got[0:32] + got[32:64] + got[64:96]
        return carry

    lax.fori_loop(0, 36, top_row, 0)
    step(0, 3)
    step(1, 1)
    begin(2)
    lax.fori_loop(36, USED, top_row, 0)
    step(0, 4)
    step(1, 2)
    begin_z(2)
    top_x()
    step_key = keys_ref[1:2, :]
    gone = ((step_key < 0) & (band == 0)) | ((step_key > 0) & (band == 31))
    mask_one = mask_one_ref[...] + jnp.where(gone, NEG, 0.0)
    for w in range(4):
        for h in range(2):
            g = (2 * w + h) * T
            bias_zero[g : g + USED, :] = top_raw[:, 8 * w + h, 0:T] + mask_zero_ref[0:USED, :]
            bias_zero[g + USED : g + T, :] = mask_zero_ref[USED:T, :]
            bias_one[g : g + USED, :] = top_raw[:, 8 * w + 2 + h, :] + mask_one[0:USED, :]
            bias_one[g + USED : g + T, :] = mask_one[USED:T, :]

    heads = heads_ref[...]
    finish(0)
    acc = jnp.zeros((T, 768), F32)
    for j in range(8):
        block = dw[j, :, :, :, 0:768].reshape(256, 768)
        acc = acc + dot(normed[:, 256 * j : 256 * j + 256], block)
    qkv = acc.astype(BF)
    mixed = attend(qkv[:, 0:256], qkv[:, 256:512], qkv[:, 512:768], deep_bias[...], heads)
    step(1, 3)
    for j in range(8):
        block = dw[j, :, :, :, 768:1024].reshape(256, 256)
        rs_send[0, j] = dot_t(mixed, block).astype(BF)
    scatter(0)
    step(2, 1)
    step(1, 4)
    column = pl.ds(pl.multiple_of(m * 256, 256), 256)
    mids[0, m] = (deep_x[:, column] + gathered_sum(0)).astype(BF)
    share(0)
    step(2, 2)
    shared(0)
    middle = jnp.concatenate([mids[0, j] for j in range(8)], axis=1).astype(F32)
    normed_two = norm_rows(middle, deep_gain_ref[1:2, :])
    finish(1)
    acc = jnp.zeros((T, 1024), F32)
    for j in range(8):
        block = dw[j, :, :, :, 1024:2048].reshape(256, 1024)
        acc = acc + dot(normed_two[:, 256 * j : 256 * j + 256], block)
    hidden = gelu(acc).astype(BF)
    step(2, 3)
    step(2, 4)
    own_skip = dot(pick_ref[x], skip_ref[...].reshape(288, 512))
    finish(2)
    for j in range(8):
        block = dw[j, :, :, :, 2048:3072].reshape(256, 1024)
        rs_send[1, j] = dot_t(hidden, block).astype(BF)
    scatter(1)
    mids[1, m] = (mids[0, m].astype(F32) + gathered_sum(1)).astype(BF)
    share(1)
    shared(1)
    acc = jnp.zeros((T, 256), F32)
    for j in range(8):
        acc = acc + dot(mids[1, j], dw[j, :, :, :, 3072:3328].reshape(256, 256))
    grown = acc.astype(BF)
    for w in range(4):
        chosen = dot(grow_ref[w], grown) * part_ref[...]
        piece = chosen[:, 0:64] + chosen[:, 64:128] + chosen[:, 128:192] + chosen[:, 192:256]
        grow_send[w] = jnp.concatenate([piece, jnp.zeros((T, 64), F32)], axis=1).astype(BF)
    for d in range(1, 8):
        send(grow_send.at[ms[d] // 2], grow_recv.at[m], s_grow.at[d - 1], r_grow.at[d - 1], at_m(d))
    grow_recv[m] = grow_send[x]
    for d in range(1, 8):
        await_at(grow_recv.at[ms[(-d) % 8]], s_grow.at[d - 1], r_grow.at[d - 1], at_m(d))
    window = jnp.concatenate([grow_recv[j][:, 0:64] for j in range(8)], axis=1)
    state = (own_skip + window.astype(F32)).astype(BF)

    for layer in range(2):
        top_ready(layer)
        base = 768 * layer
        normed = norm_rows(state.astype(F32), top_gain_ref[2 * layer : 2 * layer + 1, :])
        parts = []
        for w in range(4):
            block = tw[w, :, :, :, base : base + 256].reshape(512, 256)
            parts.append(dot(normed, block).astype(BF))
        q = jnp.concatenate([p[:, 0:64] for p in parts], axis=1)
        k = jnp.concatenate([p[:, 64:128] for p in parts], axis=1)
        v = jnp.concatenate([p[:, 128:192] for p in parts], axis=1)
        if layer == 0:
            mixed = attend(q, k, v, bias_zero[...], heads)
        else:
            kv = jnp.concatenate([k, v], axis=1)
            halo_send[...] = dot(take_ref[...], kv).astype(BF)
            halo[0:T, :] = kv
            for e, (band_step, x_step, r0, nr, c0, nc, off, size) in enumerate(PIECES):
                src = halo_send.at[pl.ds(off - T, size)]
                dst = halo.at[pl.ds(off, size)]
                send(src, dst, s_halo.at[e], r_halo.at[e], at_piece(-band_step, -x_step))
            for e, (band_step, x_step, r0, nr, c0, nc, off, size) in enumerate(PIECES):
                dst = halo.at[pl.ds(off, size)]
                await_at(dst, s_halo.at[e], r_halo.at[e], at_piece(-band_step, -x_step))
            mixed = attend(q, halo[:, 0:256], halo[:, 256:512], bias_one[...], heads)
        total = jnp.zeros((T, 512), F32)
        for w in range(4):
            block = tw[w, :, :, :, base : base + 256].reshape(512, 256)
            wide = jnp.concatenate([jnp.zeros((T, 192), BF), mixed[:, 64 * w : 64 * w + 64]], axis=1)
            total = total + dot_t(wide, block)
        swap(2 * layer, total)
        middle = (state.astype(F32) + swapped(2 * layer)).astype(BF)
        normed = norm_rows(middle.astype(F32), top_gain_ref[2 * layer + 1 : 2 * layer + 2, :])
        total = jnp.zeros((T, 512), F32)
        for w in range(4):
            block = tw[w, :, :, :, base + 256 : base + 512].reshape(512, 256)
            hidden = gelu(dot(normed, block)).astype(BF)
            total = total + dot_t(hidden, tw[w, :, :, :, base + 512 : base + 768].reshape(512, 256))
        swap(2 * layer + 1, total)
        state = (middle.astype(F32) + swapped(2 * layer + 1)).astype(BF)

    for half in range(2):
        fin[x, half] = state[:, 256 * half : 256 * half + 256]
    for d in (1, 2, 3):
        for e in range(2):
            core = lax.rem(c + e, 2)
            ss, rs = s_fin.at[d - 1, e], r_fin.at[d - 1, e]
            send(fin.at[x, c], fin.at[x, c], ss, rs, at_x(d, core))
    for d in (1, 2, 3):
        for e in range(2):
            core = lax.rem(c + e, 2)
            ss, rs = s_fin.at[d - 1, e], r_fin.at[d - 1, e]
            await_at(fin.at[xs[(-d) % 4], core], ss, rs, at_x(d, core))
    for half in range(2):
        stacked = jnp.concatenate([fin[w, half] for w in range(4)], axis=0)
        rows = dot(place_ref[...], stacked).astype(BF).reshape(6, 48, 256)
        out_ref[:, :, 256 * half : 256 * half + 256] = rows
    for cp in sends:
        cp.wait_send()


def local(
    skip_features,
    deep_features,
    top_gains,
    top_heads_in,
    top_heads_out,
    top_hidden_in,
    top_hidden_out,
    top_offsets,
    deep_gains,
    deep_offsets,
    deep_heads_in,
    deep_heads_out,
    deep_hidden_in,
    deep_hidden_out,
    expand_weight,
):
    deep_pack = jnp.concatenate(
        [
            deep_heads_in.reshape(64, 768),
            deep_heads_out.T,
            deep_hidden_in,
            deep_hidden_out.T,
            expand_weight.reshape(64, 256),
        ],
        axis=1,
    )
    top_pack = jnp.concatenate(
        [
            part
            for s in range(2)
            for part in (
                top_heads_in[s].reshape(16, 192),
                top_heads_out[s].T,
                top_hidden_in[s],
                top_hidden_out[s].T,
            )
        ],
        axis=1,
    )
    top_tab = jnp.pad(top_offsets.reshape(4, 253), ((0, 4), (0, 3)))
    deep_tab = jnp.pad(deep_offsets.reshape(8, 55), ((0, 0), (0, 73)))
    constants = [jnp.asarray(a) for a in tables()]
    operands = [
        skip_features,
        deep_features,
        top_gains.reshape(4, 512),
        deep_gains,
        top_tab,
        deep_tab,
        deep_pack,
        top_pack,
        *constants,
    ]
    dma = pltpu.SemaphoreType.DMA
    shapes = [(3, 3), (3, 7), (3, 7), (3, 8, 3), (7,), (3,), (2, 3), (3,), (2, 7), (2, 7), (7,), (4,), (8,), (3, 2)]
    vmem = pl.BlockSpec(memory_space=pltpu.VMEM)
    return pl.pallas_call(
        kernel,
        out_shape=jax.ShapeDtypeStruct((6, 48, 512), BF),
        in_specs=[vmem] * len(operands),
        out_specs=vmem,
        scratch_shapes=[
            pltpu.VMEM((8, 4, 2, 32, 3328), BF),
            pltpu.VMEM((4, 8, 4, 16, 1536), BF),
            pltpu.VMEM((4, 8, 256), F32),
            pltpu.VMEM((USED, 8, T), F32),
            pltpu.VMEM((8 * T, T), F32),
            pltpu.VMEM((USED, 32, EXT), F32),
            pltpu.VMEM((8 * T, T), F32),
            pltpu.VMEM((8 * T, EXT), F32),
            pltpu.VMEM((T, 2048), F32),
            pltpu.VMEM((2, 8, T, 256), BF),
            pltpu.VMEM((2, 8, T, 256), BF),
            pltpu.VMEM((2, 8, T, 256), BF),
            pltpu.VMEM((4, T, 128), BF),
            pltpu.VMEM((8, T, 128), BF),
            pltpu.VMEM((4, T, 512), BF),
            pltpu.VMEM((4, T, 512), BF),
            pltpu.VMEM((EXT - T, 512), BF),
            pltpu.VMEM((EXT, 512), BF),
            pltpu.VMEM((4, 2, T, 256), BF),
        ]
        + [dma(s) for s in shapes for _ in range(2)],
        compiler_params=pltpu.CompilerParams(
            collective_id=0, has_side_effects=True, vmem_limit_bytes=56 * 2**20
        ),
    )(*operands)


def solution(mesh):
    placed = (
        P("band", None, None),
        P("band", None, None),
        P(),
        P(None, "band", None, "mp"),
        P(None, "mp", "band"),
        P(None, "band", "mp"),
        P(None, "mp", "band"),
        P(None, "mp", None, None),
        P(),
        P("mp", None, None),
        P("band", None, "mp"),
        P("mp", "band"),
        P("band", "mp"),
        P("mp", "band"),
        P("band", None, "mp"),
    )
    return jax.shard_map(
        local, mesh=mesh, in_specs=placed, out_specs=P("band", None, None), check_vma=False
    )
```

time: 999 us -> 235 us (0.24)
  waiting for transfers between devices: 617 us -> 0 us
  blocking collectives: 301 us -> 0 us
  Pallas kernels: 0 us -> 224 us
  matrix products: 27.9 us -> 0 us
  other arithmetic: 14 us -> 0 us
  between operations: 14.1 us -> 0.1 us
    all_gather x5 -> x0, waiting for transfers between devices: 364 us -> none  [the longest x1 81.9 us: local(): lax.all_gather(deep_hidden_out, 'band', axis=1, tiled=True)]
    all_gather x9 -> x0, blocking collectives: 301 us -> none  [the longest x2 74.6 us: local(): lax.all_gather(top_hidden_in[section_index], 'band', axis=0, tiled=True)]
    psum x6 -> x0, waiting for transfers between devices: 250 us -> none  [the longest x2 177 us: local(): lax.psum(mlp_partial.astype(jnp.bfloat16), 'mp').astype(jnp.float32)]
    pallas_call x0 -> x1, Pallas kernels: none -> 224 us  [local(): pl.pallas_call(kernel, out_shape=jax.ShapeDtypeStruct((6, 48, 512), BF),...]
    dot_general x21 -> x0, matrix products: 26.6 us -> none  [the longest x1 6.92 us: local(): jnp.dot(deep_activated, lax.all_gather(deep_hidden_out, 'band', axis=1, t...]
  transfers between devices with their start and end apart: 13 -> 0, of which waited for: 9 -> 0; matrix products, arithmetic and copies ran while one was open for 3% -> 0% of each run, Pallas kernels for 0% -> 0%
where the time goes in v1:
time: 235 us
  Pallas kernels  224 us (95%)
  local copies, waits for them, and re-layouts  11 us (5%)
    pallas_call x1, Pallas kernels, local(): pl.pallas_call(kernel, out_shape=jax.ShapeDtypeStruct((6, 48, 512), BF),...  224 us
    unnamed x29, local copies, waits for them, and re-layouts  7.28 us

profile of v1, /device:TPU:1, one launch (start us, length us, event | category | flops | bytes accessed | tf_op | source)
XLA Modules:
  0.0 235.0 jit_solution(3720164941795816100)
XLA Ops:
  0.0 0.0 copy-start.7
  0.0 1.3 reshape.15.top_gain_ref
  1.3 0.0 copy-start.3
  1.3 0.8 copy.32
  2.1 0.1 reshape.16
  2.2 0.6 pad.8.top_tab_ref
  2.8 0.0 copy-done.7
  2.8 0.1 reshape.17
  2.9 0.6 pad.9.deep_tab_ref
  3.5 0.0 copy-done.3
  3.5 0.0 copy-start.5
  3.5 0.0 copy-start.1
  3.5 0.7 copy-done.5
  4.2 0.2 copy-done.1
  4.4 0.0 copy-start.2
  4.4 0.9 copy-done.2
  5.3 0.0 copy-start.4
  5.3 0.8 copy-done.4
  6.1 0.1 reshape.19
  6.3 0.0 copy-start.6
  6.3 0.7 copy-done.6
  7.0 0.0 copy-start
  7.0 0.0 copy-start.10
  7.0 0.0 copy-start.8
  7.0 0.1 reshape_squeeze.6
  7.1 0.6 copy-done.10
  7.8 0.1 copy-done.8
  7.8 0.0 copy-start.9
  7.9 0.7 copy-done.9
  8.6 0.1 reshape_squeeze.7
  8.7 0.7 concatenate.7.top_pack_ref
  9.4 0.0 copy-done
  9.4 223.9 %shard_map.244 = bf16[6,48,512]{2,1,0:T(8,128)(2,1)} custom-call(bf16[6,48,512]{2,1,0:T(8,128)(2,1)} %skip_ref.1, bf16[3,24,2048]{2,1,0:T(8,128)(2,1)} %deep_ref.1, f32[4,512]{1,0:T(4,128)} %reshape.15.top_gain_ref, f32[2,2048]{1,0:T(2,128)} %deep_gain_ref.1, f32[8,256]{1,0:T(8,128)} %pad.8.top_tab_ref, f32[8,128]{1,0:T(8,128)} %pad.9.deep_tab_ref, ...), custom_call_target="tpu_custom_call" | custom-call | tf_op jit(solution)/shard_map/pallas_call | solution.py:642
  233.3 1.7 copy.43
  (13 shorter events, 0.1 us)
Async XLA Ops:
  0.0 2.8 %copy-start.7 = (f32[8,5,11]{2,0,1:T(8,128)S(1)}, f32[8,5,11]{2,0,1:T(8,128)}, u32[]{:S(2)}) copy-start(f32[8,5,11]{2,0,1:T(8,128)} %param.35) | copy-start | bytes 5284
  1.3 2.1 copy-start.3
  3.5 0.8 copy-start.5
  3.5 0.9 copy-start.1
  4.4 0.9 copy-start.2
  5.3 0.8 copy-start.4
  6.3 0.7 copy-start.6
  7.0 2.4 %copy-start = (bf16[64,3328]{1,0:T(8,128)(2,1)}, bf16[64,3328]{1,0:T(8,128)(2,1)S(1)}, u32[]{:S(2)}) copy-start(bf16[64,3328]{1,0:T(8,128)(2,1)S(1)} %constant_dynamic-update-slice_fusion.deep_pack_ref) | copy-start | bytes 1277956
  7.0 0.7 copy-start.10
  7.0 0.8 copy-start.8
  7.8 0.7 copy-start.9

commit v2 on v1

v2 whole, which is shorter than its diff:
```python
import functools

import jax
import jax.numpy as jnp
import numpy as np
from jax import lax
from jax.experimental import pallas as pl
from jax.experimental.pallas import tpu as pltpu
from jax.sharding import PartitionSpec as P

BF = jnp.bfloat16
F32 = jnp.float32
EPS = 1e-05
NEG = -1e30
T = 80
USED = 72
EXT = 400
SCALE = 32 ** (-0.5)
MESH = pl.DeviceIdType.MESH
BANDS = 4

PIECES = (
    (-1, 0, 3, 3, 0, 12, 80, 48),
    (1, 0, 0, 3, 0, 12, 128, 48),
    (0, -1, 0, 6, 6, 6, 176, 48),
    (0, 1, 0, 6, 0, 6, 224, 48),
    (-1, -1, 3, 3, 6, 6, 272, 32),
    (-1, 1, 3, 3, 0, 6, 304, 32),
    (1, -1, 0, 3, 6, 6, 336, 32),
    (1, 1, 0, 3, 0, 6, 368, 32),
)


@functools.lru_cache(None)
def tables():
    key_row = np.zeros(EXT, np.int32)
    key_col = np.zeros(EXT, np.int32)
    key_ok = np.zeros(EXT, bool)
    key_step = np.zeros(EXT, np.int32)
    t = np.arange(USED)
    key_row[:USED], key_col[:USED], key_ok[:USED] = t // 12, t % 12, True
    take = np.zeros((EXT, T), np.float32)
    for band_step, x_step, r0, nr, c0, nc, off, _ in PIECES:
        p = np.arange(nr * nc)
        r, c = r0 + p // nc, c0 + p % nc
        key_row[off : off + nr * nc] = r + 6 * band_step
        key_col[off : off + nr * nc] = c + 12 * x_step
        key_ok[off : off + nr * nc] = True
        key_step[off : off + nr * nc] = band_step
        take[off + p, r * 12 + c] = 1.0
    keys = np.zeros((8, EXT), np.int32)
    keys[0] = np.where(key_ok, 23 * key_row + key_col, -100000)
    keys[1] = key_step
    q_row, q_col = np.zeros(T, np.int32), np.zeros(T, np.int32)
    q_row[:USED], q_col[:USED] = t // 12, t % 12
    same = ((q_row >= 3)[:, None] == (key_row >= 3)[None]) & (
        (q_col >= 6)[:, None] == (key_col >= 6)[None]
    )
    mask_one = np.where(same & key_ok[None], 0.0, NEG).astype(np.float32)
    mask_zero = np.where((np.arange(T) < USED)[None], 0.0, NEG).astype(np.float32)
    mask_zero = np.broadcast_to(mask_zero, (T, T)).copy()
    deep_row, deep_col = np.zeros(T, np.int32), np.zeros(T, np.int32)
    deep_row[:USED], deep_col[:USED] = t // 24, t % 24
    deep_keys = np.full((8, T), -100000, np.int32)
    deep_keys[:, :USED] = 11 * deep_row[:USED] + deep_col[:USED] % 6
    ok = (np.arange(T) < USED)[None] & ((deep_col // 6)[:, None] == (deep_col // 6)[None])
    mask_deep = np.where(ok, 0.0, NEG).astype(np.float32)
    grow = np.zeros((4, T, T), np.float32)
    part = np.zeros((T, 4), np.float32)
    i, k = t // 12, t % 12
    for w in range(4):
        grow[w, t, (i // 2) * 24 + 6 * w + k // 2] = 1.0
    part[t, 2 * (i % 2) + k % 2] = 1.0
    part = np.repeat(part[:, :, None], 64, axis=2).reshape(T, 256)
    pick = np.zeros((4, T, 288), np.float32)
    place = np.zeros((288, 4 * T), np.float32)
    for w in range(4):
        pick[w, t, i * 48 + 12 * w + k] = 1.0
        place[i * 48 + 12 * w + k, w * T + t] = 1.0
    heads = np.zeros((8 * T, 256), np.float32)
    for h in range(8):
        heads[h * T : (h + 1) * T, h * 32 : (h + 1) * 32] = 1.0
    return (
        keys,
        mask_one,
        mask_zero,
        deep_keys,
        mask_deep,
        grow.astype(jnp.bfloat16),
        part,
        pick.astype(jnp.bfloat16),
        place.astype(jnp.bfloat16),
        take[T:].astype(jnp.bfloat16),
        heads.astype(jnp.bfloat16),
    )


def dot(a, b):
    return jnp.dot(a, b, preferred_element_type=F32)


def dot_t(a, b):
    return lax.dot_general(a, b, (((1,), (1,)), ((), ())), preferred_element_type=F32)


def thirds(values):
    first = values.astype(BF)
    rest = values - first.astype(F32)
    second = rest.astype(BF)
    third = (rest - second.astype(F32)).astype(BF)
    return jnp.concatenate([first, second, third], axis=0)


def norm_rows(values, scales):
    centred = values - jnp.mean(values, axis=-1, keepdims=True)
    spread = jnp.mean(centred * centred, axis=-1, keepdims=True)
    return (centred * lax.rsqrt(spread + EPS) * scales).astype(BF)


def gelu(values):
    return values * 0.5 * (1.0 + lax.erf(values * (0.5**0.5)))


def attend(q, k, v, bias, heads):
    count = heads.shape[0] // T
    stacked = jnp.concatenate([q] * count, axis=0) * heads
    scores = dot_t(stacked, k) * SCALE + bias
    weights = jnp.exp(scores - jnp.max(scores, axis=-1, keepdims=True))
    weights = (weights * (1.0 / jnp.sum(weights, axis=-1, keepdims=True))).astype(BF)
    mixed = dot(weights, v) * heads.astype(F32)
    total = mixed[0:T]
    for h in range(1, count):
        total = total + mixed[h * T : (h + 1) * T]
    return total.astype(BF)


def kernel(
    skip_ref,
    deep_ref,
    top_gain_ref,
    deep_gain_ref,
    top_tab_ref,
    deep_tab_ref,
    heads_in_ref,
    heads_out_ref,
    hidden_in_ref,
    hidden_out_ref,
    expand_ref,
    top_heads_in_ref,
    top_heads_out_ref,
    top_hidden_in_ref,
    top_hidden_out_ref,
    keys_ref,
    mask_one_ref,
    mask_zero_ref,
    deep_keys_ref,
    mask_deep_ref,
    grow_ref,
    part_ref,
    pick_ref,
    place_ref,
    take_ref,
    heads_ref,
    out_ref,
    dw,
    quarters,
    tw,
    tabs,
    deep_raw,
    deep_bias,
    top_raw,
    bias_zero,
    bias_one,
    deep_x,
    deep_n,
    rs_send,
    rs_core,
    rs_mid,
    rs_recv,
    mids,
    outs,
    grow_send,
    grow_recv,
    swap_send,
    swap_recv,
    halo_send,
    halo,
    fin,
    s_q,
    r_q,
    s_z,
    r_z,
    s_n,
    r_n,
    s_ez,
    r_ez,
    s_ey,
    r_ey,
    s_ef,
    r_ef,
    s_tz,
    r_tz,
    s_tf,
    r_tf,
    s_tg,
    r_tg,
    s_tab,
    r_tab,
    s_core,
    r_core,
    s_rs,
    r_rs,
    s_ag,
    r_ag,
    s_mid,
    r_mid,
    s_out,
    r_out,
    s_grow,
    r_grow,
    s_swap,
    r_swap,
    s_halo,
    r_halo,
    s_fin,
    r_fin,
):
    band = lax.axis_index("band")
    m = lax.axis_index("mp")
    z, y, x, c = band // 4, band % 4, m // 2, m % 2
    zs = [lax.rem(z + d, 8) for d in range(8)]
    ys = [lax.rem(y + d, 4) for d in range(4)]
    xs = [lax.rem(x + d, 4) for d in range(4)]
    ms = [lax.rem(m + d, 8) for d in range(8)]
    other = 1 - c

    def at_z(d):
        return {"band": zs[d % 8] * 4 + y, "mp": m}

    def at_y(d):
        return {"band": z * 4 + ys[d % 4], "mp": m}

    def at_m(d):
        return {"band": band, "mp": ms[d % 8]}

    def at_plane(dx, dy):
        return {"band": z * 4 + ys[dy % 4], "mp": xs[dx % 4] * 2 + c}

    def at_x(d, core):
        return {"band": band, "mp": xs[d % 4] * 2 + core}

    def at_piece(band_step, x_step):
        return {"band": lax.rem(band + band_step + 32, 32), "mp": xs[x_step % 4] * 2 + c}

    barrier = pltpu.get_barrier_semaphore()
    greeted = [at_z(1), at_z(7)] + [at_m(d) for d in range(1, 8)]
    greeted += [at_plane(dx, dy) for dy in (1, 2, 3) for dx in range(4)]
    greeted += [at_piece(b, d) for b in (-1, 1) for d in (-1, 0, 1)]
    for who in greeted:
        pl.semaphore_signal(barrier, inc=1, device_id=who, device_id_type=MESH)

    sends = []

    def copy(src, dst, ss, rs, who):
        return pltpu.make_async_remote_copy(
            src_ref=src, dst_ref=dst, send_sem=ss, recv_sem=rs, device_id=who, device_id_type=MESH
        )

    def send(src, dst, ss, rs, who):
        cp = copy(src, dst, ss, rs, who)
        cp.start()
        sends.append(cp)

    def await_at(dst, ss, rs, who):
        copy(dst, dst, ss, rs, who).wait_recv()

    for yy in range(BANDS):
        lanes = slice(64 * yy, 64 * yy + 64)
        quarters[yy, :, 0:256] = jnp.concatenate(
            [heads_in_ref[0, :, lanes], heads_in_ref[1, :, lanes], heads_in_ref[2, :, lanes], heads_out_ref[:, lanes]],
            axis=1,
        )
        lanes = slice(256 * yy, 256 * yy + 256)
        quarters[yy, :, 256:512] = hidden_in_ref[:, lanes]
        quarters[yy, :, 512:768] = hidden_out_ref[:, lanes]
    dw[z, y, :, 0:768] = quarters[y]
    dw[z, y, :, 768:1024] = expand_ref[...]
    for layer in range(2):
        pieces = [top_heads_in_ref[layer, i] for i in range(3)] + [top_heads_out_ref[layer]]
        pieces += [top_hidden_in_ref[layer], top_hidden_out_ref[layer]]
        tw[x, z, y, :, 768 * layer : 768 * layer + 768] = jnp.concatenate(pieces, axis=1)
    tabs[x] = jnp.zeros((8, 256), F32)
    for layer in range(2):
        flat = jnp.concatenate([top_tab_ref[layer, a] for a in range(11)] + [jnp.zeros((2, 3), F32)], axis=1)
        tabs[x, 2 * layer : 2 * layer + 2, :] = flat
    pl.semaphore_wait(barrier, len(greeted))

    def plane(zz, s, part=None):
        yy = pl.ds(0, 4) if part is None else pl.ds(2 * part, 2)
        return dw.at[zz, yy, :, pl.ds(256 * s, 256)]

    def own(yy, s):
        return dw.at[z, yy, :, pl.ds(256 * s, 256)]

    def slot(way, dist):
        return dist - 1 if way > 0 else 3 + dist

    def part_of(way, dist):
        return None if dist < 4 else (0 if way > 0 else 1)

    def hop(s, way, dist):
        ref = plane(zs[(-way * (dist - 1)) % 8], s, part_of(way, dist))
        k = slot(way, dist)
        send(ref, ref, s_z.at[s, k], r_z.at[s, k], at_z(way))

    def begin(s):
        for d in (1, 3, 2):
            src = quarters.at[ys[d], :, pl.ds(256 * s, 256)]
            send(src, own(y, s), s_q.at[s, d - 1], r_q.at[s, d - 1], at_y(d))

    def begin_z(s):
        for d in (1, 3, 2):
            await_at(own(ys[(-d) % 4], s), s_q.at[s, d - 1], r_q.at[s, d - 1], at_y(d))
        hop(s, 1, 1)
        hop(s, -1, 1)

    def step(s, dist):
        for way in (1, -1):
            k = slot(way, dist)
            ref = plane(zs[(-way * dist) % 8], s, part_of(way, dist))
            await_at(ref, s_z.at[s, k], r_z.at[s, k], at_z(way))
            if dist < 4:
                hop(s, way, dist + 1)

    def expand_part(zz, part=None):
        rows = pl.ds(0, 64) if part is None else pl.ds(32 * part, 32)
        return dw.at[zz, y, rows, pl.ds(768, 256)]

    def top_part(zz, part=None):
        lanes = pl.ds(0, 1536) if part is None else pl.ds(768 * part, 768)
        return tw.at[x, zz, y, :, lanes]

    def top_hop(way, dist):
        origin, k, part = zs[(-way * (dist - 1)) % 8], slot(way, dist), part_of(way, dist)
        ref = top_part(origin, part)
        send(ref, ref, s_tz.at[k], r_tz.at[k], at_z(way))
        ref = expand_part(origin, part)
        send(ref, ref, s_ez.at[k], r_ez.at[k], at_z(way))

    def top_step(dist):
        for way in (1, -1):
            origin, k, part = zs[(-way * dist) % 8], slot(way, dist), part_of(way, dist)
            await_at(top_part(origin, part), s_tz.at[k], r_tz.at[k], at_z(way))
            await_at(expand_part(origin, part), s_ez.at[k], r_ez.at[k], at_z(way))
            if dist < 4:
                top_hop(way, dist + 1)

    def expand_of(yy, half=None):
        zz = pl.ds(0, 8) if half is None else pl.ds(4 * half, 4)
        return dw.at[zz, yy, :, pl.ds(768, 256)]

    def top_of(layer, xx, yy, half=None):
        zz = pl.ds(0, 8) if half is None else pl.ds(4 * half, 4)
        xx = pl.ds(0, 4) if xx is None else xx
        yy = pl.ds(0, 4) if yy is None else yy
        return tw.at[xx, zz, yy, :, pl.ds(768 * layer, 768)]

    def top_ref(layer, phase, d, half=None):
        along_y = (layer == 0) == (phase == 0)
        if along_y:
            return top_of(layer, x if phase == 0 else None, ys[d % 4], half)
        return top_of(layer, xs[d % 4], y if phase == 0 else None, half)

    def top_who(layer, phase, d):
        return at_y(d) if (layer == 0) == (phase == 0) else at_x(d, c)

    def top_send(layer, phase):
        ref = top_ref(layer, phase, 0)
        for e, d in enumerate((1, 3)):
            ss, rs = s_tf.at[layer, phase, e], r_tf.at[layer, phase, e]
            send(ref, ref, ss, rs, top_who(layer, phase, d))

    def top_relay(layer, phase):
        for e, d in enumerate((1, 3)):
            ss, rs = s_tf.at[layer, phase, e], r_tf.at[layer, phase, e]
            await_at(top_ref(layer, phase, -d), ss, rs, top_who(layer, phase, d))
            half = top_ref(layer, phase, -d, e)
            ss, rs = s_tg.at[layer, phase, e], r_tg.at[layer, phase, e]
            send(half, half, ss, rs, top_who(layer, phase, d))

    def top_ready(layer, phase):
        for e, d in enumerate((1, 3)):
            ss, rs = s_tg.at[layer, phase, e], r_tg.at[layer, phase, e]
            await_at(top_ref(layer, phase, 2, e), ss, rs, top_who(layer, phase, d))

    def expand_send():
        for e, d in enumerate((1, 3)):
            send(expand_of(y), expand_of(y), s_ey.at[e], r_ey.at[e], at_y(d))

    def expand_relay():
        for e, d in enumerate((1, 3)):
            yy = ys[4 - d]
            await_at(expand_of(yy), s_ey.at[e], r_ey.at[e], at_y(d))
            send(expand_of(yy, e), expand_of(yy, e), s_ef.at[e], r_ef.at[e], at_y(d))

    def expand_ready():
        for e, d in enumerate((1, 3)):
            await_at(expand_of(ys[2], e), s_ef.at[e], r_ef.at[e], at_y(d))

    steps = [(dx, dy) for dy in range(4) for dx in range(4) if dx or dy]

    def scatter(which):
        ss, rs = s_core.at[which], r_core.at[which]
        send(rs_send.at[which, other], rs_core.at[which], ss, rs, at_x(0, other))
        await_at(rs_core.at[which], ss, rs, at_x(0, other))
        rs_mid[which] = (rs_send[which, c].astype(F32) + rs_core[which].astype(F32)).astype(BF)
        for e, (dx, dy) in enumerate(steps):
            ss, rs = s_rs.at[which, e], r_rs.at[which, e]
            send(rs_mid.at[which, xs[dx], ys[dy]], rs_recv.at[which, x, y], ss, rs, at_plane(dx, dy))
        rs_recv[which, x, y] = rs_mid[which, x, y]

    def gathered_sum(which):
        for e, (dx, dy) in enumerate(steps):
            dst = rs_recv.at[which, xs[(-dx) % 4], ys[(-dy) % 4]]
            await_at(dst, s_rs.at[which, e], r_rs.at[which, e], at_plane(dx, dy))
        total = rs_recv[which, 0, 0].astype(F32)
        for j in range(1, 16):
            total = total + rs_recv[which, j // 4, j % 4].astype(F32)
        return total

    def share():
        for e, (dx, dy) in enumerate(steps):
            ref = mids.at[c, x, y]
            send(ref, ref, s_ag.at[e], r_ag.at[e], at_plane(dx, dy))

    def shared():
        for e, (dx, dy) in enumerate(steps):
            dst = mids.at[c, xs[(-dx) % 4], ys[(-dy) % 4]]
            await_at(dst, s_ag.at[e], r_ag.at[e], at_plane(dx, dy))
        send(mids.at[c], mids.at[c], s_mid.at[0], r_mid.at[0], at_x(0, other))
        await_at(mids.at[other], s_mid.at[0], r_mid.at[0], at_x(0, other))

    def share_out():
        for d in range(1, 8):
            send(outs.at[m], outs.at[m], s_out.at[d - 1], r_out.at[d - 1], at_m(d))

    def shared_out():
        for d in range(1, 8):
            await_at(outs.at[ms[(-d) % 8]], s_out.at[d - 1], r_out.at[d - 1], at_m(d))

    def swap(which, partial):
        swap_send[which] = partial.astype(BF)
        send(swap_send.at[which], swap_recv.at[which], s_swap.at[which], r_swap.at[which], at_x(0, other))

    def swapped(which):
        await_at(swap_recv.at[which], s_swap.at[which], r_swap.at[which], at_x(0, other))
        return swap_send[which].astype(F32) + swap_recv[which].astype(F32)

    begin(0)
    top_hop(1, 1)
    top_hop(-1, 1)
    for d in (1, 2, 3):
        send(tabs.at[x], tabs.at[x], s_tab.at[d - 1], r_tab.at[d - 1], at_x(d, c))

    for i in range(3):
        deep_x[24 * i : 24 * i + 24, :] = deep_ref[i].astype(F32)
    deep_x[USED:T, :] = jnp.zeros((T - USED, 2048), F32)
    deep_n[y] = norm_rows(deep_x[...], deep_gain_ref[0:1, :])
    for d in (1, 3, 2):
        send(deep_n.at[y], deep_n.at[y], s_n.at[d - 1], r_n.at[d - 1], at_y(d))
    begin(1)
    begin(2)
    begin_z(0)

    flat = jnp.concatenate([deep_tab_ref[a] for a in range(5)] + [jnp.zeros((8, 73), F32)], axis=1)
    deep_tab = thirds(flat)
    deep_iota = lax.broadcasted_iota(jnp.int32, (128, T), 0) + deep_keys_ref[0:1, :]

    def deep_rows(g, carry):
        for e in range(8):
            n = 8 * g + e
            r = n // 24
            col = n - 24 * r
            want = (r + 2) * 11 + lax.rem(col, 6) + 5
            hot = jnp.where(deep_iota == want, 1.0, 0.0).astype(BF)
            got = dot(deep_tab, hot)
            deep_raw[n] = got[0:8] + got[8:16] + got[16:24]
        return carry

    lax.fori_loop(0, 5, deep_rows, 0)
    step(0, 1)
    begin_z(1)
    top_step(1)
    lax.fori_loop(5, 9, deep_rows, 0)
    step(0, 2)
    top_step(2)
    for h in range(8):
        deep_bias[h * T : h * T + USED, :] = deep_raw[:, h, :] + mask_deep_ref[0:USED, :]
        deep_bias[h * T + USED : (h + 1) * T, :] = mask_deep_ref[USED:T, :]
    step(0, 3)
    top_step(3)
    step(1, 1)

    for d in (1, 2, 3):
        await_at(tabs.at[xs[(-d) % 4]], s_tab.at[d - 1], r_tab.at[d - 1], at_x(d, c))
    top_tab = thirds(tabs[...].reshape(32, 256))
    top_iota = lax.broadcasted_iota(jnp.int32, (256, EXT), 0) + keys_ref[0:1, :]

    def top_rows(g, carry):
        for e in range(4):
            n = 4 * g + e
            i = n // 12
            want = (i + 5) * 23 + (n - 12 * i) + 11
            hot = jnp.where(top_iota == want, 1.0, 0.0).astype(BF)
            got = dot(top_tab, hot)
            top_raw[n] = got[0:32] + got[32:64] + got[64:96]
        return carry

    step(0, 4)
    top_step(4)
    top_send(0, 0)
    top_send(1, 0)
    expand_send()
    begin_z(2)
    step(1, 2)
    for d in (1, 3, 2):
        await_at(deep_n.at[ys[(-d) % 4]], s_n.at[d - 1], r_n.at[d - 1], at_y(d))

    acc = jnp.zeros((BANDS * T, 256), F32)
    for j in range(8):
        block = dw[j, :, :, 0:256].reshape(256, 256)
        acc = acc + dot(deep_n[:, :, 256 * j : 256 * j + 256].reshape(BANDS * T, 256), block)
    qkv = acc.astype(BF)
    bias = deep_bias[pl.ds(pl.multiple_of(y * 2 * T, 2 * T), 2 * T), :]
    two = heads_ref[0 : 2 * T, 0:64]
    mixed = []
    for b in range(BANDS):
        rows = qkv[b * T : (b + 1) * T]
        mixed.append(attend(rows[:, 0:64], rows[:, 64:128], rows[:, 128:192], bias, two))
    mixed = jnp.concatenate(mixed, axis=0)
    wide = jnp.concatenate([jnp.zeros((BANDS * T, 192), BF), mixed], axis=1)
    for j in range(8):
        got = dot_t(wide, dw[j, :, :, 0:256].reshape(256, 256)).astype(BF)
        rs_send[0, j % 2, j // 2] = got.reshape(BANDS, T, 256)
    scatter(0)
    top_relay(0, 0)
    top_relay(1, 0)
    step(2, 1)
    step(1, 3)
    top_ready(0, 0)
    top_send(0, 1)
    top_ready(1, 0)
    expand_relay()
    lax.fori_loop(0, 9, top_rows, 0)
    column = pl.ds(pl.multiple_of(m * 256, 256), 256)
    mids[c, x, y] = (deep_x[:, column] + gathered_sum(0)).astype(BF)
    share()
    step(2, 2)
    step(1, 4)
    top_send(1, 1)
    step(2, 3)
    lax.fori_loop(9, 18, top_rows, 0)
    step(2, 4)
    step_key = keys_ref[1:2, :]
    gone = ((step_key < 0) & (band == 0)) | ((step_key > 0) & (band == 31))
    mask_one = mask_one_ref[...] + jnp.where(gone, NEG, 0.0)
    for w in range(4):
        for h in range(2):
            g = (2 * w + h) * T
            bias_zero[g : g + USED, :] = top_raw[:, 8 * w + h, 0:T] + mask_zero_ref[0:USED, :]
            bias_zero[g + USED : g + T, :] = mask_zero_ref[USED:T, :]
            bias_one[g : g + USED, :] = top_raw[:, 8 * w + 2 + h, :] + mask_one[0:USED, :]
            bias_one[g + USED : g + T, :] = mask_one[USED:T, :]
    heads = heads_ref[...]
    own_skip = dot(pick_ref[x], skip_ref[...].reshape(288, 512))
    shared()
    normed_two = []
    for b in range(BANDS):
        middle = jnp.concatenate([mids[j % 2, j // 2, b] for j in range(8)], axis=1).astype(F32)
        normed_two.append(norm_rows(middle, deep_gain_ref[1:2, :]))
    normed_two = jnp.concatenate(normed_two, axis=0)
    acc = jnp.zeros((BANDS * T, 256), F32)
    for j in range(8):
        block = dw[j, :, :, 256:512].reshape(256, 256)
        acc = acc + dot(normed_two[:, 256 * j : 256 * j + 256], block)
    hidden = gelu(acc).astype(BF)
    for j in range(8):
        got = dot_t(hidden, dw[j, :, :, 512:768].reshape(256, 256)).astype(BF)
        rs_send[1, j % 2, j // 2] = got.reshape(BANDS, T, 256)
    scatter(1)
    top_relay(0, 1)
    expand_ready()
    outs[m] = (mids[c, x, y].astype(F32) + gathered_sum(1)).astype(BF)
    share_out()
    top_relay(1, 1)
    shared_out()
    acc = jnp.zeros((T, 256), F32)
    for j in range(8):
        acc = acc + dot(outs[j], dw[j, :, :, 768:1024].reshape(256, 256))
    grown = acc.astype(BF)
    for w in range(4):
        chosen = dot(grow_ref[w], grown) * part_ref[...]
        piece = chosen[:, 0:64] + chosen[:, 64:128] + chosen[:, 128:192] + chosen[:, 192:256]
        grow_send[w] = jnp.concatenate([piece, jnp.zeros((T, 64), F32)], axis=1).astype(BF)
    for d in range(1, 8):
        send(grow_send.at[ms[d] // 2], grow_recv.at[m], s_grow.at[d - 1], r_grow.at[d - 1], at_m(d))
    grow_recv[m] = grow_send[x]
    for d in range(1, 8):
        await_at(grow_recv.at[ms[(-d) % 8]], s_grow.at[d - 1], r_grow.at[d - 1], at_m(d))
    window = jnp.concatenate([grow_recv[j][:, 0:64] for j in range(8)], axis=1)
    state = (own_skip + window.astype(F32)).astype(BF)

    for layer in range(2):
        top_ready(layer, 1)
        base = 768 * layer
        normed = norm_rows(state.astype(F32), top_gain_ref[layer, 0:1, :])
        parts = []
        for w in range(4):
            block = tw[w, :, :, :, base : base + 256].reshape(512, 256)
            parts.append(dot(normed, block).astype(BF))
        q = jnp.concatenate([p[:, 0:64] for p in parts], axis=1)
        k = jnp.concatenate([p[:, 64:128] for p in parts], axis=1)
        v = jnp.concatenate([p[:, 128:192] for p in parts], axis=1)
        if layer == 0:
            mixed = attend(q, k, v, bias_zero[...], heads)
        else:
            kv = jnp.concatenate([k, v], axis=1)
            halo_send[...] = dot(take_ref[...], kv).astype(BF)
            halo[0:T, :] = kv
            for e, (band_step, x_step, r0, nr, c0, nc, off, size) in enumerate(PIECES):
                src = halo_send.at[pl.ds(off - T, size)]
                dst = halo.at[pl.ds(off, size)]
                send(src, dst, s_halo.at[e], r_halo.at[e], at_piece(-band_step, -x_step))
            for e, (band_step, x_step, r0, nr, c0, nc, off, size) in enumerate(PIECES):
                dst = halo.at[pl.ds(off, size)]
                await_at(dst, s_halo.at[e], r_halo.at[e], at_piece(-band_step, -x_step))
            mixed = attend(q, halo[:, 0:256], halo[:, 256:512], bias_one[...], heads)
        total = jnp.zeros((T, 512), F32)
        for w in range(4):
            block = tw[w, :, :, :, base : base + 256].reshape(512, 256)
            wide = jnp.concatenate([jnp.zeros((T, 192), BF), mixed[:, 64 * w : 64 * w + 64]], axis=1)
            total = total + dot_t(wide, block)
        swap(2 * layer, total)
        middle = (state.astype(F32) + swapped(2 * layer)).astype(BF)
        normed = norm_rows(middle.astype(F32), top_gain_ref[layer, 1:2, :])
        total = jnp.zeros((T, 512), F32)
        for w in range(4):
            block = tw[w, :, :, :, base + 256 : base + 512].reshape(512, 256)
            hidden = gelu(dot(normed, block)).astype(BF)
            total = total + dot_t(hidden, tw[w, :, :, :, base + 512 : base + 768].reshape(512, 256))
        swap(2 * layer + 1, total)
        state = (middle.astype(F32) + swapped(2 * layer + 1)).astype(BF)

    for half in range(2):
        fin[x, half] = state[:, 256 * half : 256 * half + 256]
    for d in (1, 2, 3):
        for e in range(2):
            core = lax.rem(c + e, 2)
            ss, rs = s_fin.at[d - 1, e], r_fin.at[d - 1, e]
            send(fin.at[x, c], fin.at[x, c], ss, rs, at_x(d, core))
    for d in (1, 2, 3):
        for e in range(2):
            core = lax.rem(c + e, 2)
            ss, rs = s_fin.at[d - 1, e], r_fin.at[d - 1, e]
            await_at(fin.at[xs[(-d) % 4], core], ss, rs, at_x(d, core))
    for half in range(2):
        stacked = jnp.concatenate([fin[w, half] for w in range(4)], axis=0)
        rows = dot(place_ref[...], stacked).astype(BF).reshape(6, 48, 256)
        out_ref[:, :, 256 * half : 256 * half + 256] = rows
    for cp in sends:
        cp.wait_send()


def local(
    skip_features,
    deep_features,
    top_gains,
    top_heads_in,
    top_heads_out,
    top_hidden_in,
    top_hidden_out,
    top_offsets,
    deep_gains,
    deep_offsets,
    deep_heads_in,
    deep_heads_out,
    deep_hidden_in,
    deep_hidden_out,
    expand_weight,
):
    constants = [jnp.asarray(a) for a in tables()]
    operands = [
        skip_features,
        deep_features,
        top_gains,
        deep_gains,
        top_offsets.transpose(0, 2, 1, 3),
        deep_offsets.transpose(1, 0, 2),
        deep_heads_in.transpose(1, 0, 2),
        deep_heads_out.T,
        deep_hidden_in,
        deep_hidden_out.T,
        expand_weight.reshape(64, 256),
        top_heads_in.transpose(0, 2, 1, 3),
        top_heads_out.transpose(0, 2, 1),
        top_hidden_in,
        top_hidden_out.transpose(0, 2, 1),
        *constants,
    ]
    dma = pltpu.SemaphoreType.DMA
    shapes = [(3, 3), (3, 8), (3,), (8,), (2,), (2,), (8,), (2, 2, 2), (2, 2, 2), (3,)]
    shapes += [(2,), (2, 15), (15,), (1,), (7,), (7,), (4,), (8,), (3, 2)]
    vmem = pl.BlockSpec(memory_space=pltpu.VMEM)
    return pl.pallas_call(
        kernel,
        out_shape=jax.ShapeDtypeStruct((6, 48, 512), BF),
        in_specs=[vmem] * len(operands),
        out_specs=vmem,
        scratch_shapes=[
            pltpu.VMEM((8, 4, 64, 1024), BF),
            pltpu.VMEM((4, 64, 768), BF),
            pltpu.VMEM((4, 8, 4, 16, 1536), BF),
            pltpu.VMEM((4, 8, 256), F32),
            pltpu.VMEM((USED, 8, T), F32),
            pltpu.VMEM((8 * T, T), F32),
            pltpu.VMEM((USED, 32, EXT), F32),
            pltpu.VMEM((8 * T, T), F32),
            pltpu.VMEM((8 * T, EXT), F32),
            pltpu.VMEM((T, 2048), F32),
            pltpu.VMEM((BANDS, T, 2048), BF),
            pltpu.VMEM((2, 2, 4, BANDS, T, 256), BF),
            pltpu.VMEM((2, 4, BANDS, T, 256), BF),
            pltpu.VMEM((2, 4, BANDS, T, 256), BF),
            pltpu.VMEM((2, 4, BANDS, T, 256), BF),
            pltpu.VMEM((2, 4, BANDS, T, 256), BF),
            pltpu.VMEM((8, T, 256), BF),
            pltpu.VMEM((4, T, 128), BF),
            pltpu.VMEM((8, T, 128), BF),
            pltpu.VMEM((4, T, 512), BF),
            pltpu.VMEM((4, T, 512), BF),
            pltpu.VMEM((EXT - T, 512), BF),
            pltpu.VMEM((EXT, 512), BF),
            pltpu.VMEM((4, 2, T, 256), BF),
        ]
        + [dma(s) for s in shapes for _ in range(2)],
        compiler_params=pltpu.CompilerParams(
            collective_id=0, has_side_effects=True, vmem_limit_bytes=56 * 2**20
        ),
    )(*operands)


def solution(mesh):
    placed = (
        P("band", None, None),
        P("band", None, None),
        P(),
        P(None, "band", None, "mp"),
        P(None, "mp", "band"),
        P(None, "band", "mp"),
        P(None, "mp", "band"),
        P(None, "mp", None, None),
        P(),
        P("mp", None, None),
        P("band", None, "mp"),
        P("mp", "band"),
        P("band", "mp"),
        P("mp", "band"),
        P("band", None, "mp"),
    )
    return jax.shard_map(
        local, mesh=mesh, in_specs=placed, out_specs=P("band", None, None), check_vma=False
    )
```

time: 235 us -> 155 us (0.66)
  Pallas kernels: 224 us -> 152 us
  local copies, waits for them, and re-layouts: 11 us -> 3.26 us
    pallas_call x1, Pallas kernels: 224 us -> 152 us  [local(): pl.pallas_call(kernel, out_shape=jax.ShapeDtypeStruct((6, 48, 512), BF),...]
    unnamed x29 -> x1, local copies, waits for them, and re-layouts: 7.28 us -> 1.69 us
where the time goes in v2:
time: 155 us
  Pallas kernels  152 us (98%)
  local copies, waits for them, and re-layouts  3.26 us (2%)
    pallas_call x1, Pallas kernels, local(): pl.pallas_call(kernel, out_shape=jax.ShapeDtypeStruct((6, 48, 512), BF),...  152 us

profile of v2, /device:TPU:1, one launch (start us, length us, event | category | flops | bytes accessed | tf_op | source)
XLA Modules:
  0.0 155.2 jit_solution(18236541541690788768)
XLA Ops:
  0.0 1.6 %reshape.3.expand_ref = bf16[64,256]{1,0:T(8,128)(2,1)} reshape(bf16[64,4,64]{2,1,0:T(4,128)(2,1)} %param.40) | data formatting | bytes 65536 | tf_op jit(solution)/shard_map/reshape | solution.py:703
  1.6 152.0 %shard_map.244 = bf16[6,48,512]{2,1,0:T(8,128)(2,1)} custom-call(bf16[6,48,512]{2,1,0:T(8,128)(2,1)} %skip_ref.1, bf16[3,24,2048]{2,1,0:T(8,128)(2,1)} %deep_ref.1, f32[2,2,512]{2,1,0:T(2,128)} %top_gain_ref.1, f32[2,2048]{1,0:T(2,128)} %deep_gain_ref.1, f32[2,11,2,23]{3,2,1,0:T(2,128)} %bitcast.12, f32[5,8,11]{2,1,0:T(8,128)} %bitcast.13, ...), custom_call_target="tpu_custom_call" | custom-call | tf_op jit(solution)/shard_map/pallas_call | solution.py:714
  153.5 1.7 %copy.28 = bf16[6,48,512]{2,1,0:T(8,128)(2,1)} copy(bf16[6,48,512]{2,1,0:T(8,128)(2,1)} %shard_map.244) | data formatting | bytes 589824

commit v3 on v2

--- a/solution.py
+++ b/solution.py
@@ -200,6 +200,10 @@
     r_ef,
     s_tz,
     r_tz,
+    s_ty,
+    r_ty,
+    s_tx,
+    r_tx,
     s_tf,
     r_tf,
     s_tg,
@@ -253,9 +257,8 @@
         return {"band": lax.rem(band + band_step + 32, 32), "mp": xs[x_step % 4] * 2 + c}
 
     barrier = pltpu.get_barrier_semaphore()
-    greeted = [at_z(1), at_z(7)] + [at_m(d) for d in range(1, 8)]
-    greeted += [at_plane(dx, dy) for dy in (1, 2, 3) for dx in range(4)]
-    greeted += [at_piece(b, d) for b in (-1, 1) for d in (-1, 0, 1)]
+    greeted = [at_z(1), at_z(7), at_x(0, other)]
+    greeted += [at_y(d) for d in (1, 2, 3)] + [at_x(d, c) for d in (1, 2, 3)]
     for who in greeted:
         pl.semaphore_signal(barrier, inc=1, device_id=who, device_id_type=MESH)
 
@@ -284,7 +287,7 @@
         quarters[yy, :, 256:512] = hidden_in_ref[:, lanes]
         quarters[yy, :, 512:768] = hidden_out_ref[:, lanes]
     dw[z, y, :, 0:768] = quarters[y]
-    dw[z, y, :, 768:1024] = expand_ref[...]
+    dw[z, y, :, 768:1024] = jnp.concatenate([expand_ref[:, i, :] for i in range(4)], axis=1)
     for layer in range(2):
         pieces = [top_heads_in_ref[layer, i] for i in range(3)] + [top_heads_out_ref[layer]]
         pieces += [top_hidden_in_ref[layer], top_hidden_out_ref[layer]]
@@ -295,9 +298,11 @@
         tabs[x, 2 * layer : 2 * layer + 2, :] = flat
     pl.semaphore_wait(barrier, len(greeted))
 
-    def plane(zz, s, part=None):
-        yy = pl.ds(0, 4) if part is None else pl.ds(2 * part, 2)
-        return dw.at[zz, yy, :, pl.ds(256 * s, 256)]
+    def plane(zz, s, part):
+        some = pl.ds(2 * part, 2)
+        if s == 3:
+            return tw.at[some, zz, :, :, pl.ds(768, 768)]
+        return dw.at[zz, some, :, pl.ds(256 * s, 256)]
 
     def own(yy, s):
         return dw.at[z, yy, :, pl.ds(256 * s, 256)]
@@ -308,90 +313,127 @@
     def part_of(way, dist):
         return None if dist < 4 else (0 if way > 0 else 1)
 
-    def hop(s, way, dist):
-        ref = plane(zs[(-way * (dist - 1)) % 8], s, part_of(way, dist))
+    def limit(part, way):
+        return 4 if (part == 0) == (way > 0) else 3
+
+    def hop(s, part, way, dist):
+        ref = plane(zs[(-way * (dist - 1)) % 8], s, part)
         k = slot(way, dist)
-        send(ref, ref, s_z.at[s, k], r_z.at[s, k], at_z(way))
+        send(ref, ref, s_z.at[s, part, k], r_z.at[s, part, k], at_z(way))
+
+    def hops(s):
+        for part in range(2):
+            for way in (1, -1):
+                hop(s, part, way, 1)
 
     def begin(s):
         for d in (1, 3, 2):
             src = quarters.at[ys[d], :, pl.ds(256 * s, 256)]
             send(src, own(y, s), s_q.at[s, d - 1], r_q.at[s, d - 1], at_y(d))
 
+    def second(yy=None, xx=None):
+        return tw.at[x if xx is None else xx, z, pl.ds(0, 4) if yy is None else yy, :, pl.ds(768, 768)]
+
+    def second_y():
+        for d in (1, 3, 2):
+            send(second(y), second(y), s_ty.at[d - 1], r_ty.at[d - 1], at_y(d))
+
+    def second_x():
+        for d in (1, 3, 2):
+            await_at(second(ys[(-d) % 4]), s_ty.at[d - 1], r_ty.at[d - 1], at_y(d))
+        for d in (1, 3, 2):
+            send(second(), second(), s_tx.at[d - 1], r_tx.at[d - 1], at_x(d, c))
+
+    def second_z():
+        for d in (1, 3, 2):
+            await_at(second(None, xs[(-d) % 4]), s_tx.at[d - 1], r_tx.at[d - 1], at_x(d, c))
+        hops(3)
+
     def begin_z(s):
         for d in (1, 3, 2):
             await_at(own(ys[(-d) % 4], s), s_q.at[s, d - 1], r_q.at[s, d - 1], at_y(d))
-        hop(s, 1, 1)
-        hop(s, -1, 1)
+        hops(s)
 
     def step(s, dist):
-        for way in (1, -1):
-            k = slot(way, dist)
-            ref = plane(zs[(-way * dist) % 8], s, part_of(way, dist))
-            await_at(ref, s_z.at[s, k], r_z.at[s, k], at_z(way))
-            if dist < 4:
-                hop(s, way, dist + 1)
+        for part in range(2):
+            for way in (1, -1):
+                if dist > limit(part, way):
+                    continue
+                k = slot(way, dist)
+                ref = plane(zs[(-way * dist) % 8], s, part)
+                await_at(ref, s_z.at[s, part, k], r_z.at[s, part, k], at_z(way))
+                if dist < limit(part, way):
+                    hop(s, part, way, dist + 1)
 
     def expand_part(zz, part=None):
         rows = pl.ds(0, 64) if part is None else pl.ds(32 * part, 32)
         return dw.at[zz, y, rows, pl.ds(768, 256)]
 
     def top_part(zz, part=None):
-        lanes = pl.ds(0, 1536) if part is None else pl.ds(768 * part, 768)
+        lanes = pl.ds(0, 768) if part is None else pl.ds(384 * part, 384)
         return tw.at[x, zz, y, :, lanes]
 
     def top_hop(way, dist):
         origin, k, part = zs[(-way * (dist - 1)) % 8], slot(way, dist), part_of(way, dist)
         ref = top_part(origin, part)
         send(ref, ref, s_tz.at[k], r_tz.at[k], at_z(way))
-        ref = expand_part(origin, part)
-        send(ref, ref, s_ez.at[k], r_ez.at[k], at_z(way))
 
     def top_step(dist):
         for way in (1, -1):
             origin, k, part = zs[(-way * dist) % 8], slot(way, dist), part_of(way, dist)
             await_at(top_part(origin, part), s_tz.at[k], r_tz.at[k], at_z(way))
+            if dist < 4:
+                top_hop(way, dist + 1)
+
+    def expand_hop(way, dist):
+        origin, k, part = zs[(-way * (dist - 1)) % 8], slot(way, dist), part_of(way, dist)
+        ref = expand_part(origin, part)
+        send(ref, ref, s_ez.at[k], r_ez.at[k], at_z(way))
+
+    def expand_step(dist):
+        for way in (1, -1):
+            origin, k, part = zs[(-way * dist) % 8], slot(way, dist), part_of(way, dist)
             await_at(expand_part(origin, part), s_ez.at[k], r_ez.at[k], at_z(way))
             if dist < 4:
-                top_hop(way, dist + 1)
+                expand_hop(way, dist + 1)
 
     def expand_of(yy, half=None):
         zz = pl.ds(0, 8) if half is None else pl.ds(4 * half, 4)
         return dw.at[zz, yy, :, pl.ds(768, 256)]
 
-    def top_of(layer, xx, yy, half=None):
+    def top_of(half_of, xx, yy, half=None):
         zz = pl.ds(0, 8) if half is None else pl.ds(4 * half, 4)
         xx = pl.ds(0, 4) if xx is None else xx
         yy = pl.ds(0, 4) if yy is None else yy
-        return tw.at[xx, zz, yy, :, pl.ds(768 * layer, 768)]
-
-    def top_ref(layer, phase, d, half=None):
-        along_y = (layer == 0) == (phase == 0)
+        return tw.at[xx, zz, yy, :, pl.ds(384 * half_of, 384)]
+
+    def top_ref(half_of, phase, d, half=None):
+        along_y = (half_of == 0) == (phase == 0)
         if along_y:
-            return top_of(layer, x if phase == 0 else None, ys[d % 4], half)
-        return top_of(layer, xs[d % 4], y if phase == 0 else None, half)
-
-    def top_who(layer, phase, d):
-        return at_y(d) if (layer == 0) == (phase == 0) else at_x(d, c)
-
-    def top_send(layer, phase):
-        ref = top_ref(layer, phase, 0)
+            return top_of(half_of, x if phase == 0 else None, ys[d % 4], half)
+        return top_of(half_of, xs[d % 4], y if phase == 0 else None, half)
+
+    def top_who(half_of, phase, d):
+        return at_y(d) if (half_of == 0) == (phase == 0) else at_x(d, c)
+
+    def top_send(half_of, phase):
+        ref = top_ref(half_of, phase, 0)
         for e, d in enumerate((1, 3)):
-            ss, rs = s_tf.at[layer, phase, e], r_tf.at[layer, phase, e]
-            send(ref, ref, ss, rs, top_who(layer, phase, d))
-
-    def top_relay(layer, phase):
+            ss, rs = s_tf.at[half_of, phase, e], r_tf.at[half_of, phase, e]
+            send(ref, ref, ss, rs, top_who(half_of, phase, d))
+
+    def top_relay(half_of, phase):
         for e, d in enumerate((1, 3)):
-            ss, rs = s_tf.at[layer, phase, e], r_tf.at[layer, phase, e]
-            await_at(top_ref(layer, phase, -d), ss, rs, top_who(layer, phase, d))
-            half = top_ref(layer, phase, -d, e)
-            ss, rs = s_tg.at[layer, phase, e], r_tg.at[layer, phase, e]
-            send(half, half, ss, rs, top_who(layer, phase, d))
-
-    def top_ready(layer, phase):
+            ss, rs = s_tf.at[half_of, phase, e], r_tf.at[half_of, phase, e]
+            await_at(top_ref(half_of, phase, -d), ss, rs, top_who(half_of, phase, d))
+            half = top_ref(half_of, phase, -d, e)
+            ss, rs = s_tg.at[half_of, phase, e], r_tg.at[half_of, phase, e]
+            send(half, half, ss, rs, top_who(half_of, phase, d))
+
+    def top_ready(half_of, phase):
         for e, d in enumerate((1, 3)):
-            ss, rs = s_tg.at[layer, phase, e], r_tg.at[layer, phase, e]
-            await_at(top_ref(layer, phase, 2, e), ss, rs, top_who(layer, phase, d))
+            ss, rs = s_tg.at[half_of, phase, e], r_tg.at[half_of, phase, e]
+            await_at(top_ref(half_of, phase, 2, e), ss, rs, top_who(half_of, phase, d))
 
     def expand_send():
         for e, d in enumerate((1, 3)):
@@ -408,15 +450,22 @@
             await_at(expand_of(ys[2], e), s_ef.at[e], r_ef.at[e], at_y(d))
 
     steps = [(dx, dy) for dy in range(4) for dx in range(4) if dx or dy]
+    steps.sort(key=lambda d: min(d[0], 4 - d[0]) + min(d[1], 4 - d[1]))
 
     def scatter(which):
-        ss, rs = s_core.at[which], r_core.at[which]
-        send(rs_send.at[which, other], rs_core.at[which], ss, rs, at_x(0, other))
-        await_at(rs_core.at[which], ss, rs, at_x(0, other))
-        rs_mid[which] = (rs_send[which, c].astype(F32) + rs_core[which].astype(F32)).astype(BF)
-        for e, (dx, dy) in enumerate(steps):
-            ss, rs = s_rs.at[which, e], r_rs.at[which, e]
-            send(rs_mid.at[which, xs[dx], ys[dy]], rs_recv.at[which, x, y], ss, rs, at_plane(dx, dy))
+        order = (2, 1, 3, 0)
+        for dx in order:
+            ss, rs = s_core.at[which, dx], r_core.at[which, dx]
+            send(rs_send.at[which, other, xs[dx]], rs_core.at[which, xs[dx]], ss, rs, at_x(0, other))
+        for dx in order:
+            ss, rs = s_core.at[which, dx], r_core.at[which, dx]
+            await_at(rs_core.at[which, xs[dx]], ss, rs, at_x(0, other))
+            both = rs_send[which, c, xs[dx]].astype(F32) + rs_core[which, xs[dx]].astype(F32)
+            rs_mid[which, xs[dx]] = both.astype(BF)
+            for e, (ex, dy) in enumerate(steps):
+                if ex == dx:
+                    ss, rs = s_rs.at[which, e], r_rs.at[which, e]
+                    send(rs_mid.at[which, xs[dx], ys[dy]], rs_recv.at[which, x, y], ss, rs, at_plane(dx, dy))
         rs_recv[which, x, y] = rs_mid[which, x, y]
 
     def gathered_sum(which):
@@ -428,17 +477,23 @@
             total = total + rs_recv[which, j // 4, j % 4].astype(F32)
         return total
 
+    def pass_mid(ref, e):
+        send(ref, ref, s_mid.at[e], r_mid.at[e], at_x(0, other))
+
     def share():
         for e, (dx, dy) in enumerate(steps):
             ref = mids.at[c, x, y]
             send(ref, ref, s_ag.at[e], r_ag.at[e], at_plane(dx, dy))
+        pass_mid(mids.at[c, x, y], 15)
 
     def shared():
         for e, (dx, dy) in enumerate(steps):
             dst = mids.at[c, xs[(-dx) % 4], ys[(-dy) % 4]]
             await_at(dst, s_ag.at[e], r_ag.at[e], at_plane(dx, dy))
-        send(mids.at[c], mids.at[c], s_mid.at[0], r_mid.at[0], at_x(0, other))
-        await_at(mids.at[other], s_mid.at[0], r_mid.at[0], at_x(0, other))
+            pass_mid(dst, e)
+        for e, (dx, dy) in enumerate(steps + [(0, 0)]):
+            dst = mids.at[other, xs[(-dx) % 4], ys[(-dy) % 4]]
+            await_at(dst, s_mid.at[e], r_mid.at[e], at_x(0, other))
 
     def share_out():
         for d in range(1, 8):
@@ -459,6 +514,7 @@
     begin(0)
     top_hop(1, 1)
     top_hop(-1, 1)
+    second_y()
     for d in (1, 2, 3):
         send(tabs.at[x], tabs.at[x], s_tab.at[d - 1], r_tab.at[d - 1], at_x(d, c))
 
@@ -468,9 +524,11 @@
     deep_n[y] = norm_rows(deep_x[...], deep_gain_ref[0:1, :])
     for d in (1, 3, 2):
         send(deep_n.at[y], deep_n.at[y], s_n.at[d - 1], r_n.at[d - 1], at_y(d))
+
     begin(1)
     begin(2)
     begin_z(0)
+    top_step(1)
 
     flat = jnp.concatenate([deep_tab_ref[a] for a in range(5)] + [jnp.zeros((8, 73), F32)], axis=1)
     deep_tab = thirds(flat)
@@ -487,19 +545,24 @@
             deep_raw[n] = got[0:8] + got[8:16] + got[16:24]
         return carry
 
-    lax.fori_loop(0, 5, deep_rows, 0)
     step(0, 1)
+    top_step(2)
+    second_x()
+    lax.fori_loop(0, 4, deep_rows, 0)
+    step(0, 2)
+    top_step(3)
+    lax.fori_loop(4, 9, deep_rows, 0)
+    step(0, 3)
     begin_z(1)
-    top_step(1)
-    lax.fori_loop(5, 9, deep_rows, 0)
-    step(0, 2)
-    top_step(2)
+    begin_z(2)
+    expand_hop(1, 1)
+    expand_hop(-1, 1)
+    top_step(4)
+    top_send(0, 0)
+    top_send(1, 0)
     for h in range(8):
         deep_bias[h * T : h * T + USED, :] = deep_raw[:, h, :] + mask_deep_ref[0:USED, :]
         deep_bias[h * T + USED : (h + 1) * T, :] = mask_deep_ref[USED:T, :]
-    step(0, 3)
-    top_step(3)
-    step(1, 1)
 
     for d in (1, 2, 3):
         await_at(tabs.at[xs[(-d) % 4]], s_tab.at[d - 1], r_tab.at[d - 1], at_x(d, c))
@@ -516,13 +579,8 @@
             top_raw[n] = got[0:32] + got[32:64] + got[64:96]
         return carry
 
+    lax.fori_loop(0, 6, top_rows, 0)
     step(0, 4)
-    top_step(4)
-    top_send(0, 0)
-    top_send(1, 0)
-    expand_send()
-    begin_z(2)
-    step(1, 2)
     for d in (1, 3, 2):
         await_at(deep_n.at[ys[(-d) % 4]], s_n.at[d - 1], r_n.at[d - 1], at_y(d))
 
@@ -545,22 +603,25 @@
     scatter(0)
     top_relay(0, 0)
     top_relay(1, 0)
+    step(1, 1)
     step(2, 1)
-    step(1, 3)
+    expand_step(1)
+    lax.fori_loop(6, 12, top_rows, 0)
+    step(1, 2)
+    step(2, 2)
+    expand_step(2)
+    column = pl.ds(pl.multiple_of(m * 256, 256), 256)
+    mids[c, x, y] = (deep_x[:, column] + gathered_sum(0)).astype(BF)
+    share()
     top_ready(0, 0)
     top_send(0, 1)
     top_ready(1, 0)
-    expand_relay()
-    lax.fori_loop(0, 9, top_rows, 0)
-    column = pl.ds(pl.multiple_of(m * 256, 256), 256)
-    mids[c, x, y] = (deep_x[:, column] + gathered_sum(0)).astype(BF)
-    share()
-    step(2, 2)
-    step(1, 4)
     top_send(1, 1)
+    step(1, 3)
     step(2, 3)
-    lax.fori_loop(9, 18, top_rows, 0)
-    step(2, 4)
+    expand_step(3)
+    second_z()
+    lax.fori_loop(12, 18, top_rows, 0)
     step_key = keys_ref[1:2, :]
     gone = ((step_key < 0) & (band == 0)) | ((step_key > 0) & (band == 31))
     mask_one = mask_one_ref[...] + jnp.where(gone, NEG, 0.0)
@@ -573,6 +634,10 @@
             bias_one[g + USED : g + T, :] = mask_one[USED:T, :]
     heads = heads_ref[...]
     own_skip = dot(pick_ref[x], skip_ref[...].reshape(288, 512))
+    step(1, 4)
+    step(2, 4)
+    expand_step(4)
+    expand_send()
     shared()
     normed_two = []
     for b in range(BANDS):
@@ -589,10 +654,13 @@
         rs_send[1, j % 2, j // 2] = got.reshape(BANDS, T, 256)
     scatter(1)
     top_relay(0, 1)
-    expand_ready()
+    top_relay(1, 1)
+    expand_relay()
+    step(3, 1)
     outs[m] = (mids[c, x, y].astype(F32) + gathered_sum(1)).astype(BF)
     share_out()
-    top_relay(1, 1)
+    step(3, 2)
+    expand_ready()
     shared_out()
     acc = jnp.zeros((T, 256), F32)
     for j in range(8):
@@ -604,6 +672,7 @@
         grow_send[w] = jnp.concatenate([piece, jnp.zeros((T, 64), F32)], axis=1).astype(BF)
     for d in range(1, 8):
         send(grow_send.at[ms[d] // 2], grow_recv.at[m], s_grow.at[d - 1], r_grow.at[d - 1], at_m(d))
+    step(3, 3)
     grow_recv[m] = grow_send[x]
     for d in range(1, 8):
         await_at(grow_recv.at[ms[(-d) % 8]], s_grow.at[d - 1], r_grow.at[d - 1], at_m(d))
@@ -611,7 +680,11 @@
     state = (own_skip + window.astype(F32)).astype(BF)
 
     for layer in range(2):
-        top_ready(layer, 1)
+        if layer == 0:
+            top_ready(0, 1)
+            top_ready(1, 1)
+        else:
+            step(3, 4)
         base = 768 * layer
         normed = norm_rows(state.astype(F32), top_gain_ref[layer, 0:1, :])
         parts = []
@@ -700,7 +773,7 @@
         deep_heads_out.T,
         deep_hidden_in,
         deep_hidden_out.T,
-        expand_weight.reshape(64, 256),
+        expand_weight,
         top_heads_in.transpose(0, 2, 1, 3),
         top_heads_out.transpose(0, 2, 1),
         top_hidden_in,
@@ -708,8 +781,8 @@
         *constants,
     ]
     dma = pltpu.SemaphoreType.DMA
-    shapes = [(3, 3), (3, 8), (3,), (8,), (2,), (2,), (8,), (2, 2, 2), (2, 2, 2), (3,)]
-    shapes += [(2,), (2, 15), (15,), (1,), (7,), (7,), (4,), (8,), (3, 2)]
+    shapes = [(3, 3), (4, 2, 8), (3,), (8,), (2,), (2,), (8,), (3,), (3,), (2, 2, 2), (2, 2, 2), (3,)]
+    shapes += [(2, 4), (2, 15), (15,), (16,), (7,), (7,), (4,), (8,), (3, 2)]
     vmem = pl.BlockSpec(memory_space=pltpu.VMEM)
     return pl.pallas_call(
         kernel,

time: 155 us -> 128 us (0.83)
  Pallas kernels: 152 us -> 126 us
  local copies, waits for them, and re-layouts: 3.26 us -> 1.69 us
    pallas_call x1, Pallas kernels: 152 us -> 126 us  [local(): pl.pallas_call(kernel, out_shape=jax.ShapeDtypeStruct((6, 48, 512), BF),...]
    reshape x1 -> x0, local copies, waits for them, and re-layouts: 1.57 us -> none  [local(): expand_weight.reshape(64, 256)]
where the time goes in v3:
time: 128 us
  Pallas kernels  126 us (98%)
  local copies, waits for them, and re-layouts  1.69 us (1%)
    pallas_call x1, Pallas kernels, local(): pl.pallas_call(kernel, out_shape=jax.ShapeDtypeStruct((6, 48, 512), BF),...  126 us

profile of v3, /device:TPU:1, one launch (start us, length us, event | category | flops | bytes accessed | tf_op | source)
XLA Modules:
  0.0 128.0 jit_solution(10574770703492701062)
XLA Ops:
  0.0 126.3 %shard_map.244 = bf16[6,48,512]{2,1,0:T(8,128)(2,1)} custom-call(bf16[6,48,512]{2,1,0:T(8,128)(2,1)} %skip_ref.1, bf16[3,24,2048]{2,1,0:T(8,128)(2,1)} %deep_ref.1, f32[2,2,512]{2,1,0:T(2,128)} %top_gain_ref.1, f32[2,2048]{1,0:T(2,128)} %deep_gain_ref.1, f32[2,11,2,23]{3,2,1,0:T(2,128)} %bitcast.12, f32[5,8,11]{2,1,0:T(8,128)} %bitcast.13, ...), custom_call_target="tpu_custom_call" | custom-call | tf_op jit(solution)/shard_map/pallas_call | solution.py:787
  126.3 1.7 %copy.28 = bf16[6,48,512]{2,1,0:T(8,128)(2,1)} copy(bf16[6,48,512]{2,1,0:T(8,128)(2,1)} %shard_map.244) | data formatting | bytes 589824

commit v4 on v3

--- a/solution.py
+++ b/solution.py
@@ -17,7 +17,7 @@
 EXT = 400
 SCALE = 32 ** (-0.5)
 MESH = pl.DeviceIdType.MESH
-BANDS = 4
+BANDS = 2
 
 PIECES = (
     (-1, 0, 3, 3, 0, 12, 80, 48),
@@ -166,6 +166,7 @@
     quarters,
     tw,
     tabs,
+    deep_tabs,
     deep_raw,
     deep_bias,
     top_raw,
@@ -174,9 +175,8 @@
     deep_x,
     deep_n,
     rs_send,
-    rs_core,
-    rs_mid,
     rs_recv,
+    own_mid,
     mids,
     outs,
     grow_send,
@@ -210,14 +210,14 @@
     r_tg,
     s_tab,
     r_tab,
-    s_core,
-    r_core,
+    s_f,
+    r_f,
+    s_dt,
+    r_dt,
     s_rs,
     r_rs,
     s_ag,
     r_ag,
-    s_mid,
-    r_mid,
     s_out,
     r_out,
     s_grow,
@@ -274,10 +274,20 @@
         cp.start()
         sends.append(cp)
 
+    conditional = []
+
+    def send_if(cond, src, dst, ss, rs, who):
+        cp = copy(src, dst, ss, rs, who)
+        pl.when(cond)(cp.start)
+        conditional.append((cond, cp))
+
+    def await_if(cond, dst, ss, rs, who):
+        pl.when(cond)(copy(dst, dst, ss, rs, who).wait_recv)
+
     def await_at(dst, ss, rs, who):
         copy(dst, dst, ss, rs, who).wait_recv()
 
-    for yy in range(BANDS):
+    for yy in range(4):
         lanes = slice(64 * yy, 64 * yy + 64)
         quarters[yy, :, 0:256] = jnp.concatenate(
             [heads_in_ref[0, :, lanes], heads_in_ref[1, :, lanes], heads_in_ref[2, :, lanes], heads_out_ref[:, lanes]],
@@ -286,12 +296,14 @@
         lanes = slice(256 * yy, 256 * yy + 256)
         quarters[yy, :, 256:512] = hidden_in_ref[:, lanes]
         quarters[yy, :, 512:768] = hidden_out_ref[:, lanes]
-    dw[z, y, :, 0:768] = quarters[y]
-    dw[z, y, :, 768:1024] = jnp.concatenate([expand_ref[:, i, :] for i in range(4)], axis=1)
+    dw[c, z, y, :, 0:768] = quarters[y]
+    dw[c, z, y, :, 768:1024] = jnp.concatenate([expand_ref[:, i, :] for i in range(4)], axis=1)
     for layer in range(2):
         pieces = [top_heads_in_ref[layer, i] for i in range(3)] + [top_heads_out_ref[layer]]
         pieces += [top_hidden_in_ref[layer], top_hidden_out_ref[layer]]
         tw[x, z, y, :, 768 * layer : 768 * layer + 768] = jnp.concatenate(pieces, axis=1)
+    flat = jnp.concatenate([deep_tab_ref[a] for a in range(5)] + [jnp.zeros((8, 73), F32)], axis=1)
+    deep_tabs[c] = flat
     tabs[x] = jnp.zeros((8, 256), F32)
     for layer in range(2):
         flat = jnp.concatenate([top_tab_ref[layer, a] for a in range(11)] + [jnp.zeros((2, 3), F32)], axis=1)
@@ -302,10 +314,10 @@
         some = pl.ds(2 * part, 2)
         if s == 3:
             return tw.at[some, zz, :, :, pl.ds(768, 768)]
-        return dw.at[zz, some, :, pl.ds(256 * s, 256)]
+        return dw.at[c, zz, some, :, pl.ds(256 * s, 256)]
 
     def own(yy, s):
-        return dw.at[z, yy, :, pl.ds(256 * s, 256)]
+        return dw.at[c, z, yy, :, pl.ds(256 * s, 256)]
 
     def slot(way, dist):
         return dist - 1 if way > 0 else 3 + dist
@@ -325,6 +337,20 @@
         for part in range(2):
             for way in (1, -1):
                 hop(s, part, way, 1)
+
+    def forward(s, zz, part, k):
+        if s < 3:
+            ref = plane(zz, s, part)
+            send(ref, ref, s_f.at[s, part, k], r_f.at[s, part, k], at_x(0, other))
+
+    def finish(s):
+        for part in range(2):
+            for way, most in ((0, 1), (1, limit(part, 1)), (-1, limit(part, -1))):
+                for dist in range(1, most + 1):
+                    k = 8 if way == 0 else slot(way, dist)
+                    zz = zs[(-way * dist) % 8]
+                    ref = dw.at[other, zz, pl.ds(2 * part, 2), :, pl.ds(256 * s, 256)]
+                    await_at(ref, s_f.at[s, part, k], r_f.at[s, part, k], at_x(0, other))
 
     def begin(s):
         for d in (1, 3, 2):
@@ -353,6 +379,8 @@
         for d in (1, 3, 2):
             await_at(own(ys[(-d) % 4], s), s_q.at[s, d - 1], r_q.at[s, d - 1], at_y(d))
         hops(s)
+        for part in range(2):
+            forward(s, z, part, 8)
 
     def step(s, dist):
         for part in range(2):
@@ -364,10 +392,11 @@
                 await_at(ref, s_z.at[s, part, k], r_z.at[s, part, k], at_z(way))
                 if dist < limit(part, way):
                     hop(s, part, way, dist + 1)
+                forward(s, zs[(-way * dist) % 8], part, k)
 
     def expand_part(zz, part=None):
         rows = pl.ds(0, 64) if part is None else pl.ds(32 * part, 32)
-        return dw.at[zz, y, rows, pl.ds(768, 256)]
+        return dw.at[c, zz, y, rows, pl.ds(768, 256)]
 
     def top_part(zz, part=None):
         lanes = pl.ds(0, 768) if part is None else pl.ds(384 * part, 384)
@@ -399,7 +428,7 @@
 
     def expand_of(yy, half=None):
         zz = pl.ds(0, 8) if half is None else pl.ds(4 * half, 4)
-        return dw.at[zz, yy, :, pl.ds(768, 256)]
+        return dw.at[c, zz, yy, :, pl.ds(768, 256)]
 
     def top_of(half_of, xx, yy, half=None):
         zz = pl.ds(0, 8) if half is None else pl.ds(4 * half, 4)
@@ -451,49 +480,54 @@
 
     steps = [(dx, dy) for dy in range(4) for dx in range(4) if dx or dy]
     steps.sort(key=lambda d: min(d[0], 4 - d[0]) + min(d[1], 4 - d[1]))
+    keeper = y // 2
+    sibling = at_x(0, other)
 
     def scatter(which):
-        order = (2, 1, 3, 0)
-        for dx in order:
-            ss, rs = s_core.at[which, dx], r_core.at[which, dx]
-            send(rs_send.at[which, other, xs[dx]], rs_core.at[which, xs[dx]], ss, rs, at_x(0, other))
-        for dx in order:
-            ss, rs = s_core.at[which, dx], r_core.at[which, dx]
-            await_at(rs_core.at[which, xs[dx]], ss, rs, at_x(0, other))
-            both = rs_send[which, c, xs[dx]].astype(F32) + rs_core[which, xs[dx]].astype(F32)
-            rs_mid[which, xs[dx]] = both.astype(BF)
-            for e, (ex, dy) in enumerate(steps):
-                if ex == dx:
-                    ss, rs = s_rs.at[which, e], r_rs.at[which, e]
-                    send(rs_mid.at[which, xs[dx], ys[dy]], rs_recv.at[which, x, y], ss, rs, at_plane(dx, dy))
-        rs_recv[which, x, y] = rs_mid[which, x, y]
+        for d in (4, 3, 5, 2, 6, 1, 7, 0):
+            for b in range(2):
+                src, dst = rs_send.at[which, b, ms[d]], rs_recv.at[which, x, y]
+                ss, rs = s_rs.at[which, 8 * b + d], r_rs.at[which, 4 * x + y]
+                who = {"band": z * 4 + 2 * c + b, "mp": ms[d]}
+                if d:
+                    send(src, dst, ss, rs, who)
+                else:
+                    send_if(y != 2 * c + b, src, dst, ss, rs, who)
+
+        @pl.when(c == keeper)
+        def _():
+            rs_recv[which, x, y] = rs_send[which, y % 2, m]
 
     def gathered_sum(which):
-        for e, (dx, dy) in enumerate(steps):
-            dst = rs_recv.at[which, xs[(-dx) % 4], ys[(-dy) % 4]]
-            await_at(dst, s_rs.at[which, e], r_rs.at[which, e], at_plane(dx, dy))
+        await_if(c != keeper, rs_recv.at[which, x, y], s_rs.at[which, 0], r_rs.at[which, 4 * x + y], sibling)
+        for dx, dy in steps:
+            xx, yy = xs[(-dx) % 4], ys[(-dy) % 4]
+            await_at(rs_recv.at[which, xx, yy], s_rs.at[which, 0], r_rs.at[which, 4 * xx + yy], sibling)
         total = rs_recv[which, 0, 0].astype(F32)
         for j in range(1, 16):
             total = total + rs_recv[which, j // 4, j % 4].astype(F32)
         return total
 
-    def pass_mid(ref, e):
-        send(ref, ref, s_mid.at[e], r_mid.at[e], at_x(0, other))
-
     def share():
-        for e, (dx, dy) in enumerate(steps):
-            ref = mids.at[c, x, y]
-            send(ref, ref, s_ag.at[e], r_ag.at[e], at_plane(dx, dy))
-        pass_mid(mids.at[c, x, y], 15)
+        dst, rs = mids.at[y % 2, m], r_ag.at[8 * (y % 2) + m]
+        for e, (dx, dy) in reversed(list(enumerate(steps))):
+            who = {"band": z * 4 + ys[dy], "mp": 2 * xs[dx] + keeper}
+            send(own_mid, dst, s_ag.at[e], rs, who)
+        send_if(c != keeper, own_mid, dst, s_ag.at[15], rs, sibling)
+
+        @pl.when(c == keeper)
+        def _():
+            mids[y % 2, m] = own_mid[...]
 
     def shared():
-        for e, (dx, dy) in enumerate(steps):
-            dst = mids.at[c, xs[(-dx) % 4], ys[(-dy) % 4]]
-            await_at(dst, s_ag.at[e], r_ag.at[e], at_plane(dx, dy))
-            pass_mid(dst, e)
-        for e, (dx, dy) in enumerate(steps + [(0, 0)]):
-            dst = mids.at[other, xs[(-dx) % 4], ys[(-dy) % 4]]
-            await_at(dst, s_mid.at[e], r_mid.at[e], at_x(0, other))
+        for d in range(8):
+            for b in range(2):
+                j = ms[(-d) % 8]
+                dst, ss, rs = mids.at[b, j], s_ag.at[0], r_ag.at[8 * b + j]
+                if d:
+                    await_at(dst, ss, rs, sibling)
+                else:
+                    await_if(y != 2 * c + b, dst, ss, rs, sibling)
 
     def share_out():
         for d in range(1, 8):
@@ -514,7 +548,10 @@
     begin(0)
     top_hop(1, 1)
     top_hop(-1, 1)
+    expand_hop(1, 1)
+    expand_hop(-1, 1)
     second_y()
+    send(deep_tabs.at[c], deep_tabs.at[c], s_dt.at[0], r_dt.at[0], sibling)
     for d in (1, 2, 3):
         send(tabs.at[x], tabs.at[x], s_tab.at[d - 1], r_tab.at[d - 1], at_x(d, c))
 
@@ -523,15 +560,18 @@
     deep_x[USED:T, :] = jnp.zeros((T - USED, 2048), F32)
     deep_n[y] = norm_rows(deep_x[...], deep_gain_ref[0:1, :])
     for d in (1, 3, 2):
-        send(deep_n.at[y], deep_n.at[y], s_n.at[d - 1], r_n.at[d - 1], at_y(d))
+        send_if(c == keeper, deep_n.at[y], deep_n.at[y], s_n.at[d - 1], r_n.at[y], at_y(d))
+
 
     begin(1)
     begin(2)
+    top_step(1)
+    expand_step(1)
     begin_z(0)
-    top_step(1)
-
-    flat = jnp.concatenate([deep_tab_ref[a] for a in range(5)] + [jnp.zeros((8, 73), F32)], axis=1)
-    deep_tab = thirds(flat)
+    top_step(2)
+    expand_step(2)
+    await_at(deep_tabs.at[other], s_dt.at[0], r_dt.at[0], sibling)
+    deep_tab = thirds(deep_tabs[...].reshape(16, 128))
     deep_iota = lax.broadcasted_iota(jnp.int32, (128, T), 0) + deep_keys_ref[0:1, :]
 
     def deep_rows(g, carry):
@@ -542,25 +582,27 @@
             want = (r + 2) * 11 + lax.rem(col, 6) + 5
             hot = jnp.where(deep_iota == want, 1.0, 0.0).astype(BF)
             got = dot(deep_tab, hot)
-            deep_raw[n] = got[0:8] + got[8:16] + got[16:24]
+            deep_raw[n] = got[0:16] + got[16:32] + got[32:48]
         return carry
 
     step(0, 1)
-    top_step(2)
+    top_step(3)
+    expand_step(3)
     second_x()
     lax.fori_loop(0, 4, deep_rows, 0)
     step(0, 2)
-    top_step(3)
+    top_step(4)
+    expand_step(4)
+    top_send(0, 0)
+    top_send(1, 0)
+    expand_send()
     lax.fori_loop(4, 9, deep_rows, 0)
     step(0, 3)
     begin_z(1)
     begin_z(2)
-    expand_hop(1, 1)
-    expand_hop(-1, 1)
-    top_step(4)
-    top_send(0, 0)
-    top_send(1, 0)
-    for h in range(8):
+    top_relay(0, 0)
+    top_relay(1, 0)
+    for h in range(16):
         deep_bias[h * T : h * T + USED, :] = deep_raw[:, h, :] + mask_deep_ref[0:USED, :]
         deep_bias[h * T + USED : (h + 1) * T, :] = mask_deep_ref[USED:T, :]
 
@@ -581,37 +623,39 @@
 
     lax.fori_loop(0, 6, top_rows, 0)
     step(0, 4)
-    for d in (1, 3, 2):
-        await_at(deep_n.at[ys[(-d) % 4]], s_n.at[d - 1], r_n.at[d - 1], at_y(d))
-
-    acc = jnp.zeros((BANDS * T, 256), F32)
+    expand_relay()
+    for b in range(2):
+        yy = 2 * c + b
+        await_if(y != yy, deep_n.at[yy], s_n.at[0], r_n.at[yy], sibling)
+
+    finish(0)
+    two = heads_ref[0 : 2 * T, 0:64]
+    out = [0.0] * 8
+    for e in range(2):
+        acc = jnp.zeros((BANDS * T, 256), F32)
+        for j in range(8):
+            rows = deep_n[pl.ds(2 * c, 2), :, 256 * j : 256 * j + 256].reshape(BANDS * T, 256)
+            acc = acc + dot(rows, dw[e, j, :, :, 0:256].reshape(256, 256))
+        qkv = acc.astype(BF)
+        bias = deep_bias[pl.ds(pl.multiple_of((8 * e + 2 * y) * T, 2 * T), 2 * T), :]
+        mixed = []
+        for b in range(BANDS):
+            rows = qkv[b * T : (b + 1) * T]
+            mixed.append(attend(rows[:, 0:64], rows[:, 64:128], rows[:, 128:192], bias, two))
+        mixed = jnp.concatenate(mixed, axis=0)
+        wide = jnp.concatenate([jnp.zeros((BANDS * T, 192), BF), mixed], axis=1)
+        for j in range(8):
+            out[j] = out[j] + dot_t(wide, dw[e, j, :, :, 0:256].reshape(256, 256))
     for j in range(8):
-        block = dw[j, :, :, 0:256].reshape(256, 256)
-        acc = acc + dot(deep_n[:, :, 256 * j : 256 * j + 256].reshape(BANDS * T, 256), block)
-    qkv = acc.astype(BF)
-    bias = deep_bias[pl.ds(pl.multiple_of(y * 2 * T, 2 * T), 2 * T), :]
-    two = heads_ref[0 : 2 * T, 0:64]
-    mixed = []
-    for b in range(BANDS):
-        rows = qkv[b * T : (b + 1) * T]
-        mixed.append(attend(rows[:, 0:64], rows[:, 64:128], rows[:, 128:192], bias, two))
-    mixed = jnp.concatenate(mixed, axis=0)
-    wide = jnp.concatenate([jnp.zeros((BANDS * T, 192), BF), mixed], axis=1)
-    for j in range(8):
-        got = dot_t(wide, dw[j, :, :, 0:256].reshape(256, 256)).astype(BF)
-        rs_send[0, j % 2, j // 2] = got.reshape(BANDS, T, 256)
+        rs_send[0, :, j] = out[j].astype(BF).reshape(BANDS, T, 256)
     scatter(0)
-    top_relay(0, 0)
-    top_relay(1, 0)
     step(1, 1)
     step(2, 1)
-    expand_step(1)
     lax.fori_loop(6, 12, top_rows, 0)
     step(1, 2)
     step(2, 2)
-    expand_step(2)
     column = pl.ds(pl.multiple_of(m * 256, 256), 256)
-    mids[c, x, y] = (deep_x[:, column] + gathered_sum(0)).astype(BF)
+    own_mid[...] = (deep_x[:, column] + gathered_sum(0)).astype(BF)
     share()
     top_ready(0, 0)
     top_send(0, 1)
@@ -619,7 +663,6 @@
     top_send(1, 1)
     step(1, 3)
     step(2, 3)
-    expand_step(3)
     second_z()
     lax.fori_loop(12, 18, top_rows, 0)
     step_key = keys_ref[1:2, :]
@@ -636,35 +679,37 @@
     own_skip = dot(pick_ref[x], skip_ref[...].reshape(288, 512))
     step(1, 4)
     step(2, 4)
-    expand_step(4)
-    expand_send()
     shared()
     normed_two = []
     for b in range(BANDS):
-        middle = jnp.concatenate([mids[j % 2, j // 2, b] for j in range(8)], axis=1).astype(F32)
+        middle = jnp.concatenate([mids[b, j] for j in range(8)], axis=1).astype(F32)
         normed_two.append(norm_rows(middle, deep_gain_ref[1:2, :]))
     normed_two = jnp.concatenate(normed_two, axis=0)
-    acc = jnp.zeros((BANDS * T, 256), F32)
+    finish(1)
+    finish(2)
+    out = [0.0] * 8
+    for e in range(2):
+        acc = jnp.zeros((BANDS * T, 256), F32)
+        for j in range(8):
+            block = dw[e, j, :, :, 256:512].reshape(256, 256)
+            acc = acc + dot(normed_two[:, 256 * j : 256 * j + 256], block)
+        hidden = gelu(acc).astype(BF)
+        for j in range(8):
+            out[j] = out[j] + dot_t(hidden, dw[e, j, :, :, 512:768].reshape(256, 256))
     for j in range(8):
-        block = dw[j, :, :, 256:512].reshape(256, 256)
-        acc = acc + dot(normed_two[:, 256 * j : 256 * j + 256], block)
-    hidden = gelu(acc).astype(BF)
-    for j in range(8):
-        got = dot_t(hidden, dw[j, :, :, 512:768].reshape(256, 256)).astype(BF)
-        rs_send[1, j % 2, j // 2] = got.reshape(BANDS, T, 256)
+        rs_send[1, :, j] = out[j].astype(BF).reshape(BANDS, T, 256)
     scatter(1)
     top_relay(0, 1)
     top_relay(1, 1)
-    expand_relay()
     step(3, 1)
-    outs[m] = (mids[c, x, y].astype(F32) + gathered_sum(1)).astype(BF)
+    outs[m] = (own_mid[...].astype(F32) + gathered_sum(1)).astype(BF)
     share_out()
     step(3, 2)
     expand_ready()
     shared_out()
     acc = jnp.zeros((T, 256), F32)
     for j in range(8):
-        acc = acc + dot(outs[j], dw[j, :, :, 768:1024].reshape(256, 256))
+        acc = acc + dot(outs[j], dw[c, j, :, :, 768:1024].reshape(256, 256))
     grown = acc.astype(BF)
     for w in range(4):
         chosen = dot(grow_ref[w], grown) * part_ref[...]
@@ -742,6 +787,8 @@
         out_ref[:, :, 256 * half : 256 * half + 256] = rows
     for cp in sends:
         cp.wait_send()
+    for cond, cp in conditional:
+        pl.when(cond)(cp.wait_send)
 
 
 def local(
@@ -781,8 +828,8 @@
         *constants,
     ]
     dma = pltpu.SemaphoreType.DMA
-    shapes = [(3, 3), (4, 2, 8), (3,), (8,), (2,), (2,), (8,), (3,), (3,), (2, 2, 2), (2, 2, 2), (3,)]
-    shapes += [(2, 4), (2, 15), (15,), (16,), (7,), (7,), (4,), (8,), (3, 2)]
+    shapes = [(3, 3), (4, 2, 8), (4,), (8,), (2,), (2,), (8,), (3,), (3,), (2, 2, 2), (2, 2, 2), (3,)]
+    shapes += [(3, 2, 9), (1,), (2, 16), (16,), (7,), (7,), (4,), (8,), (3, 2)]
     vmem = pl.BlockSpec(memory_space=pltpu.VMEM)
     return pl.pallas_call(
         kernel,
@@ -790,22 +837,22 @@
         in_specs=[vmem] * len(operands),
         out_specs=vmem,
         scratch_shapes=[
-            pltpu.VMEM((8, 4, 64, 1024), BF),
+            pltpu.VMEM((2, 8, 4, 64, 1024), BF),
             pltpu.VMEM((4, 64, 768), BF),
             pltpu.VMEM((4, 8, 4, 16, 1536), BF),
             pltpu.VMEM((4, 8, 256), F32),
-            pltpu.VMEM((USED, 8, T), F32),
-            pltpu.VMEM((8 * T, T), F32),
+            pltpu.VMEM((2, 8, 128), F32),
+            pltpu.VMEM((USED, 16, T), F32),
+            pltpu.VMEM((16 * T, T), F32),
             pltpu.VMEM((USED, 32, EXT), F32),
             pltpu.VMEM((8 * T, T), F32),
             pltpu.VMEM((8 * T, EXT), F32),
             pltpu.VMEM((T, 2048), F32),
-            pltpu.VMEM((BANDS, T, 2048), BF),
-            pltpu.VMEM((2, 2, 4, BANDS, T, 256), BF),
-            pltpu.VMEM((2, 4, BANDS, T, 256), BF),
-            pltpu.VMEM((2, 4, BANDS, T, 256), BF),
-            pltpu.VMEM((2, 4, BANDS, T, 256), BF),
-            pltpu.VMEM((2, 4, BANDS, T, 256), BF),
+            pltpu.VMEM((4, T, 2048), BF),
+            pltpu.VMEM((2, BANDS, 8, T, 256), BF),
+            pltpu.VMEM((2, 4, 4, T, 256), BF),
+            pltpu.VMEM((T, 256), BF),
+            pltpu.VMEM((BANDS, 8, T, 256), BF),
             pltpu.VMEM((8, T, 256), BF),
             pltpu.VMEM((4, T, 128), BF),
             pltpu.VMEM((8, T, 128), BF),

time: 128 us -> 119 us (0.930)
  Pallas kernels: 126 us -> 117 us
    pallas_call x1, Pallas kernels: 126 us -> 117 us  [local(): pl.pallas_call(kernel, out_shape=jax.ShapeDtypeStruct((6, 48, 512), BF),...]
where the time goes in v4:
time: 119 us
  Pallas kernels  117 us (98%)
  local copies, waits for them, and re-layouts  1.69 us (1%)
    pallas_call x1, Pallas kernels, local(): pl.pallas_call(kernel, out_shape=jax.ShapeDtypeStruct((6, 48, 512), BF),...  117 us

profile of v4, /device:TPU:1, one launch (start us, length us, event | category | flops | bytes accessed | tf_op | source)
XLA Modules:
  0.0 118.6 jit_solution(4294992165153451390)
XLA Ops:
  0.0 116.9 %shard_map.244 = bf16[6,48,512]{2,1,0:T(8,128)(2,1)} custom-call(bf16[6,48,512]{2,1,0:T(8,128)(2,1)} %skip_ref.1, bf16[3,24,2048]{2,1,0:T(8,128)(2,1)} %deep_ref.1, f32[2,2,512]{2,1,0:T(2,128)} %top_gain_ref.1, f32[2,2048]{1,0:T(2,128)} %deep_gain_ref.1, f32[2,11,2,23]{3,2,1,0:T(2,128)} %bitcast.12, f32[5,8,11]{2,1,0:T(8,128)} %bitcast.13, ...), custom_call_target="tpu_custom_call" | custom-call | tf_op jit(solution)/shard_map/pallas_call | solution.py:834
  116.9 1.7 %copy.28 = bf16[6,48,512]{2,1,0:T(8,128)(2,1)} copy(bf16[6,48,512]{2,1,0:T(8,128)(2,1)} %shard_map.244) | data formatting | bytes 589824

commit v5 on v4

--- a/solution.py
+++ b/solution.py
@@ -657,10 +657,6 @@
     column = pl.ds(pl.multiple_of(m * 256, 256), 256)
     own_mid[...] = (deep_x[:, column] + gathered_sum(0)).astype(BF)
     share()
-    top_ready(0, 0)
-    top_send(0, 1)
-    top_ready(1, 0)
-    top_send(1, 1)
     step(1, 3)
     step(2, 3)
     second_z()
@@ -679,6 +675,10 @@
     own_skip = dot(pick_ref[x], skip_ref[...].reshape(288, 512))
     step(1, 4)
     step(2, 4)
+    top_ready(0, 0)
+    top_send(0, 1)
+    top_ready(1, 0)
+    top_send(1, 1)
     shared()
     normed_two = []
     for b in range(BANDS):
@@ -699,11 +699,11 @@
     for j in range(8):
         rs_send[1, :, j] = out[j].astype(BF).reshape(BANDS, T, 256)
     scatter(1)
-    top_relay(0, 1)
-    top_relay(1, 1)
     step(3, 1)
     outs[m] = (own_mid[...].astype(F32) + gathered_sum(1)).astype(BF)
     share_out()
+    top_relay(0, 1)
+    top_relay(1, 1)
     step(3, 2)
     expand_ready()
     shared_out()
@@ -727,7 +727,6 @@
     for layer in range(2):
         if layer == 0:
             top_ready(0, 1)
-            top_ready(1, 1)
         else:
             step(3, 4)
         base = 768 * layer
@@ -759,6 +758,8 @@
             wide = jnp.concatenate([jnp.zeros((T, 192), BF), mixed[:, 64 * w : 64 * w + 64]], axis=1)
             total = total + dot_t(wide, block)
         swap(2 * layer, total)
+        if layer == 0:
+            top_ready(1, 1)
         middle = (state.astype(F32) + swapped(2 * layer)).astype(BF)
         normed = norm_rows(middle.astype(F32), top_gain_ref[layer, 1:2, :])
         total = jnp.zeros((T, 512), F32)

time: 119 us -> 117 us (0.983)
  Pallas kernels: 117 us -> 115 us
    pallas_call x1, Pallas kernels: 117 us -> 115 us  [local(): pl.pallas_call(kernel, out_shape=jax.ShapeDtypeStruct((6, 48, 512), BF),...]
where the time goes in v5:
time: 117 us
  Pallas kernels  115 us (98%)
  local copies, waits for them, and re-layouts  1.69 us (1%)
    pallas_call x1, Pallas kernels, local(): pl.pallas_call(kernel, out_shape=jax.ShapeDtypeStruct((6, 48, 512), BF),...  115 us

profile of v5, /device:TPU:1, one launch (start us, length us, event | category | flops | bytes accessed | tf_op | source)
XLA Modules:
  0.0 117.1 jit_solution(3283048611497548883)
XLA Ops:
  0.0 115.4 %shard_map.244 = bf16[6,48,512]{2,1,0:T(8,128)(2,1)} custom-call(bf16[6,48,512]{2,1,0:T(8,128)(2,1)} %skip_ref.1, bf16[3,24,2048]{2,1,0:T(8,128)(2,1)} %deep_ref.1, f32[2,2,512]{2,1,0:T(2,128)} %top_gain_ref.1, f32[2,2048]{1,0:T(2,128)} %deep_gain_ref.1, f32[2,11,2,23]{3,2,1,0:T(2,128)} %bitcast.12, f32[5,8,11]{2,1,0:T(8,128)} %bitcast.13, ...), custom_call_target="tpu_custom_call" | custom-call | tf_op jit(solution)/shard_map/pallas_call | solution.py:835
  115.4 1.7 %copy.28 = bf16[6,48,512]{2,1,0:T(8,128)(2,1)} copy(bf16[6,48,512]{2,1,0:T(8,128)(2,1)} %shard_map.244) | data formatting | bytes 589824

commit v6 on v5

--- a/solution.py
+++ b/solution.py
@@ -17,6 +17,7 @@
 EXT = 400
 SCALE = 32 ** (-0.5)
 MESH = pl.DeviceIdType.MESH
+FETCHED = (0, 16, 20, 21, 22, 23, 24, 25)
 BANDS = 2
 
 PIECES = (
@@ -135,7 +136,7 @@
 
 
 def kernel(
-    skip_ref,
+    skip_hbm,
     deep_ref,
     top_gain_ref,
     deep_gain_ref,
@@ -151,16 +152,16 @@
     top_hidden_in_ref,
     top_hidden_out_ref,
     keys_ref,
-    mask_one_ref,
+    mask_one_hbm,
     mask_zero_ref,
     deep_keys_ref,
     mask_deep_ref,
-    grow_ref,
-    part_ref,
-    pick_ref,
-    place_ref,
-    take_ref,
-    heads_ref,
+    grow_hbm,
+    part_hbm,
+    pick_hbm,
+    place_hbm,
+    take_hbm,
+    heads_hbm,
     out_ref,
     dw,
     quarters,
@@ -186,6 +187,15 @@
     halo_send,
     halo,
     fin,
+    skip_ref,
+    mask_one_ref,
+    grow_ref,
+    part_ref,
+    pick_ref,
+    place_ref,
+    take_ref,
+    heads_ref,
+    s_fetch,
     s_q,
     r_q,
     s_z,
@@ -256,6 +266,20 @@
     def at_piece(band_step, x_step):
         return {"band": lax.rem(band + band_step + 32, 32), "mp": xs[x_step % 4] * 2 + c}
 
+    fetched = [
+        (skip_hbm, skip_ref),
+        (mask_one_hbm, mask_one_ref),
+        (grow_hbm, grow_ref),
+        (part_hbm, part_ref),
+        (pick_hbm, pick_ref),
+        (place_hbm, place_ref),
+        (take_hbm, take_ref),
+        (heads_hbm, heads_ref),
+    ]
+    fetched = [pltpu.make_async_copy(a, b, s_fetch.at[i]) for i, (a, b) in enumerate(fetched)]
+    for cp in fetched:
+        cp.start()
+
     barrier = pltpu.get_barrier_semaphore()
     greeted = [at_z(1), at_z(7), at_x(0, other)]
     greeted += [at_y(d) for d in (1, 2, 3)] + [at_x(d, c) for d in (1, 2, 3)]
@@ -555,6 +579,8 @@
     for d in (1, 2, 3):
         send(tabs.at[x], tabs.at[x], s_tab.at[d - 1], r_tab.at[d - 1], at_x(d, c))
 
+    for cp in fetched:
+        cp.wait()
     for i in range(3):
         deep_x[24 * i : 24 * i + 24, :] = deep_ref[i].astype(F32)
     deep_x[USED:T, :] = jnp.zeros((T - USED, 2048), F32)
@@ -598,8 +624,6 @@
     expand_send()
     lax.fori_loop(4, 9, deep_rows, 0)
     step(0, 3)
-    begin_z(1)
-    begin_z(2)
     top_relay(0, 0)
     top_relay(1, 0)
     for h in range(16):
@@ -628,6 +652,8 @@
         yy = 2 * c + b
         await_if(y != yy, deep_n.at[yy], s_n.at[0], r_n.at[yy], sibling)
 
+    begin_z(1)
+    begin_z(2)
     finish(0)
     two = heads_ref[0 : 2 * T, 0:64]
     out = [0.0] * 8
@@ -832,10 +858,11 @@
     shapes = [(3, 3), (4, 2, 8), (4,), (8,), (2,), (2,), (8,), (3,), (3,), (2, 2, 2), (2, 2, 2), (3,)]
     shapes += [(3, 2, 9), (1,), (2, 16), (16,), (7,), (7,), (4,), (8,), (3, 2)]
     vmem = pl.BlockSpec(memory_space=pltpu.VMEM)
+    hbm = pl.BlockSpec(memory_space=pl.ANY)
     return pl.pallas_call(
         kernel,
         out_shape=jax.ShapeDtypeStruct((6, 48, 512), BF),
-        in_specs=[vmem] * len(operands),
+        in_specs=[hbm if i in FETCHED else vmem for i in range(len(operands))],
         out_specs=vmem,
         scratch_shapes=[
             pltpu.VMEM((2, 8, 4, 64, 1024), BF),
@@ -863,6 +890,8 @@
             pltpu.VMEM((EXT, 512), BF),
             pltpu.VMEM((4, 2, T, 256), BF),
         ]
+        + [pltpu.VMEM(operands[i].shape, operands[i].dtype) for i in FETCHED]
+        + [dma((len(FETCHED),))]
         + [dma(s) for s in shapes for _ in range(2)],
         compiler_params=pltpu.CompilerParams(
             collective_id=0, has_side_effects=True, vmem_limit_bytes=56 * 2**20

time: 117 us -> 116 us (level)
    pallas_call x1, Pallas kernels: 115 us -> 114 us  [local(): pl.pallas_call(kernel, out_shape=jax.ShapeDtypeStruct((6, 48, 512), BF),...]
where the time goes in v6:
time: 116 us
  Pallas kernels  114 us (98%)
  local copies, waits for them, and re-layouts  1.69 us (1%)
    pallas_call x1, Pallas kernels, local(): pl.pallas_call(kernel, out_shape=jax.ShapeDtypeStruct((6, 48, 512), BF),...  114 us

profile of v6, /device:TPU:1, one launch (start us, length us, event | category | flops | bytes accessed | tf_op | source)
XLA Modules:
  0.0 115.7 jit_solution(16593178513956305466)
XLA Ops:
  0.0 114.0 %shard_map.244 = bf16[6,48,512]{2,1,0:T(8,128)(2,1)} custom-call(bf16[6,48,512]{2,1,0:T(8,128)(2,1)} %skip_hbm.1, bf16[3,24,2048]{2,1,0:T(8,128)(2,1)} %deep_ref.1, f32[2,2,512]{2,1,0:T(2,128)} %top_gain_ref.1, f32[2,2048]{1,0:T(2,128)} %deep_gain_ref.1, f32[2,11,2,23]{3,2,1,0:T(2,128)} %bitcast.12, f32[5,8,11]{2,1,0:T(8,128)} %bitcast.13, ...), custom_call_target="tpu_custom_call" | custom-call | tf_op jit(solution)/shard_map/pallas_call | solution.py:862
  114.0 1.7 %copy.28 = bf16[6,48,512]{2,1,0:T(8,128)(2,1)} copy(bf16[6,48,512]{2,1,0:T(8,128)(2,1)} %shard_map.244) | data formatting | bytes 589824
